TPU v7x, 32 devices: a whole 2x2x4 slice. The times are simulated.
32 devices in a mesh: dp: 8 (over z, y), mp: 4 (over x, core).
Axes of the slice: x: 2, y: 2, z: 4, core: 2. Of those that a mesh axis runs over, the one named last changes fastest.
Arguments:
- tokens: bfloat16 [50176, 512], P(('dp', 'mp')), may hold values from -6 to 6
- regions: int32 [128, 392], P('dp'), may hold values from 0 to 7, as said below
- first_gain: float32 [512], P('dp'), may hold values from 0.5 to 1.5
- first_shift: float32 [512], P('dp'), may hold values from -4 to 4
- triple_weight: float32 [3, 512, 512], P(None, 'dp', 'mp'), may hold values from -0.375 to 0.375
- query_bias: float32 [512], P('dp'), may hold values from -6 to 6
- value_bias: float32 [512], P('dp'), may hold values from -6 to 6
- offset_table: float32 [16, 2535], P('mp'), may hold values from -6 to 6
- output_weight: float32 [512, 512], P('mp', 'dp'), may hold values from -1 to 1
- output_bias: float32 [512], P('dp'), may hold values from -4 to 4
- second_gain: float32 [512], P('dp'), may hold values from 0.5 to 1.5
- second_shift: float32 [512], P('dp'), may hold values from -4 to 4
- inner_weight: float32 [512, 2048], P('dp', 'mp'), may hold values from -0.25 to 0.25
- inner_bias: float32 [2048], P('dp'), may hold values from -6 to 6
- outer_weight: float32 [2048, 512], P('mp', 'dp'), may hold values from -0.1875 to 0.1875
- outer_bias: float32 [512], P('dp'), may hold values from -4 to 4
- cotangent: bfloat16 [50176, 512], P(('dp', 'mp')), may hold values from -6 to 6
Outputs:
- result: bfloat16 [50176, 512], P(('dp', 'mp'))
- gradient_tokens: bfloat16 [50176, 512], P(('dp', 'mp'))
- gradient_first_gain: float32 [512], P(('dp', 'mp'))
- gradient_first_shift: float32 [512], P(('dp', 'mp'))
- gradient_triple: float32 [3, 512, 512], P(None, 'dp', 'mp')
- gradient_query_bias: float32 [512], P(('dp', 'mp'))
- gradient_value_bias: float32 [512], P(('dp', 'mp'))
- gradient_offsets: float32 [16, 2535], P('mp')
- gradient_output_weight: float32 [512, 512], P('mp', 'dp')
- gradient_output_bias: float32 [512], P(('dp', 'mp'))
- gradient_second_gain: float32 [512], P(('dp', 'mp'))
- gradient_second_shift: float32 [512], P(('dp', 'mp'))
- gradient_inner_weight: float32 [512, 2048], P('dp', 'mp')
- gradient_inner_bias: float32 [2048], P(('dp', 'mp'))
- gradient_outer_weight: float32 [2048, 512], P('mp', 'dp')
- gradient_outer_bias: float32 [512], P(('dp', 'mp'))
- head_maxima: float32 [16], P('mp')
- clipped_weight: float32 [2, 512, 512], P(None, 'dp', 'mp')
Inputs may be any that keep to these rules, and one draw needn't show every extreme that they name: `regions`: for each window there are cut points 0 <= c_t < 8, 0 <= c_h < 7, 0 <= c_w < 7, and the id of the token at place (t, h, w) is 4 * [t >= c_t] + 2 * [h >= c_h] + [w >= c_w]; windows 7, 15, 23 and so on are cut at (4, 3, 3).
All inputs are finite; a program needn't handle non-finite values.
Results may differ from a plain program's by a relative error of at most 0.02.
Values may be sent and summed in bfloat16 or wider, within the bound.
No kernel may reach another device: no remote copies, remote signals or barrier semaphores. Data moves between devices by JAX's collectives and lax.ppermute only.
A program may use at most 192 MiB of HBM per device.

v0:
```python
import math

import jax
import jax.numpy as jnp
from jax import lax
from jax.sharding import PartitionSpec as P

D = 512
HEADS = 16
HEAD_DIM = 32
FF = 2048
WIN_T = 8
WIN_H = 7
WIN_W = 7
WIN_BLOCK = 2
WIN = 392
TABLE = 2535


norm_epsilon = 1e-05
masked_score = -1000000000.0
clip_target = 10.0
root_half = 0.7071067811865476
density_scale = 0.3989422804014327
highest_precision = lax.Precision.HIGHEST


def combined_all(value, axis, join):
    gathered = jax.tree.map(
        lambda a, kind: lax.all_gather(a.astype(kind), axis),
        value,
        (
            jnp.bfloat16,
            jnp.bfloat16,
            jnp.bfloat16,
            jnp.bfloat16,
            jnp.bfloat16,
            jnp.bfloat16,
            jnp.bfloat16,
            jnp.bfloat16,
            jnp.bfloat16,
            jnp.bfloat16,
            jnp.bfloat16,
        ),
    )

    def take(source):
        return jax.tree.map(
            lambda a, own: lax.dynamic_index_in_dim(a, source, 0, False).astype(own.dtype),
            gathered,
            value,
        )

    return lax.fori_loop(
        1, lax.axis_size(axis), lambda source, state: join(state, take(source)), take(0)
    )


def product(left, right):
    return jnp.dot(left, right, preferred_element_type=jnp.float32)


def product_transposed(left, right):
    return lax.dot_general(
        left, right, (((1,), (1,)), ((), ())), preferred_element_type=jnp.float32
    )


def contract_rows(left, right):
    return lax.dot_general(
        left, right, (((0,), (0,)), ((), ())), preferred_element_type=jnp.float32
    )


def norm_forward(values, norm_gain, norm_shift):
    centred = values - jnp.mean(values, axis=1, keepdims=True)
    inverse = lax.rsqrt(jnp.mean(centred * centred, axis=1, keepdims=True) + norm_epsilon)
    scaled = centred * inverse
    return (scaled * norm_gain + norm_shift, scaled, inverse)


def norm_backward(upstream, scaled, inverse, norm_gain):
    along = upstream * norm_gain
    return inverse * (
        along
        - jnp.mean(along, axis=1, keepdims=True)
        - scaled * jnp.mean(along * scaled, axis=1, keepdims=True)
    )


def gelu_slope(values):
    return (
        0.5 * (1.0 + lax.erf(values * root_half))
        + values * jnp.exp(-0.5 * values * values) * density_scale
    )


def offset_matches():
    time_places = jnp.arange(WIN_T)
    time_offset = time_places[:, None] - time_places[None, :] + WIN_T - 1
    time_match = (time_offset[:, :, None] == jnp.arange(2 * WIN_T - 1)[None, None, :]).astype(
        jnp.float32
    )
    space_places = jnp.arange(WIN_H * WIN_W)
    along_height = space_places // WIN_W
    along_width = space_places % WIN_W
    space_offset = (along_height[:, None] - along_height[None, :] + WIN_H - 1) * (2 * WIN_W - 1) + (
        along_width[:, None] - along_width[None, :] + WIN_W - 1
    )
    space_match = (
        space_offset[:, :, None] == jnp.arange((2 * WIN_H - 1) * (2 * WIN_W - 1))[None, None, :]
    ).astype(jnp.float32)
    return (time_match, space_match)


def build_grid(table_here, time_match, space_match):
    heads_here = table_here.shape[0]
    folded = table_here.reshape(heads_here, 2 * WIN_T - 1, (2 * WIN_H - 1) * (2 * WIN_W - 1))
    spatial = jnp.einsum("hab,klb->hakl", folded, space_match, precision=highest_precision)
    grid = jnp.einsum("hakl,ija->hikjl", spatial, time_match, precision=highest_precision)
    return grid.reshape(heads_here, WIN, WIN)


def reduce_grid(grid_grad, time_match, space_match):
    heads_here = grid_grad.shape[0]
    unfolded = grid_grad.reshape(heads_here, WIN_T, WIN_H * WIN_W, WIN_T, WIN_H * WIN_W)
    by_time = jnp.einsum("hikjl,ija->hakl", unfolded, time_match, precision=highest_precision)
    table_grad = jnp.einsum("hakl,klb->hab", by_time, space_match, precision=highest_precision)
    return table_grad.reshape(heads_here, TABLE)


def attend_forward(queries, key_rows, value_rows, regions_here, bias_grid, windows_block):
    heads_here = bias_grid.shape[0]
    blocks = regions_here.shape[0] // windows_block
    split_shape = (blocks, windows_block, WIN, heads_here, HEAD_DIM)
    score_scale = 1.0 / math.sqrt(HEAD_DIM)

    def one_block(inputs):
        block_queries, block_keys, block_values, block_regions = inputs
        allowed = (block_regions[:, :, None] == block_regions[:, None, :])[:, None]
        scores = (
            jnp.einsum(
                "wihd,wjhd->whij", block_queries, block_keys, preferred_element_type=jnp.float32
            )
            * score_scale
        )
        block_max = jnp.max(scores, axis=(0, 2, 3))
        logits = jnp.where(allowed, scores + bias_grid[None], masked_score)
        highest = jnp.max(logits, axis=3, keepdims=True)
        raised = jnp.exp(logits - highest)
        totals = jnp.sum(raised, axis=3, keepdims=True)
        weights_soft = (raised / totals).astype(jnp.bfloat16)
        mixed = jnp.einsum(
            "whij,wjhd->wihd", weights_soft, block_values, preferred_element_type=jnp.float32
        )
        return (mixed.astype(jnp.bfloat16), (highest + jnp.log(totals))[..., 0], block_max)

    mixed, log_totals, maxima = lax.map(
        one_block,
        (
            queries.reshape(split_shape),
            key_rows.reshape(split_shape),
            value_rows.reshape(split_shape),
            regions_here.reshape(blocks, windows_block, WIN),
        ),
    )
    return (mixed.reshape(queries.shape), log_totals, jnp.max(maxima, axis=0))


def attend_backward(
    queries, key_rows, value_rows, regions_here, bias_grid, log_totals, attended_grad, windows_block
):
    heads_here = bias_grid.shape[0]
    blocks = regions_here.shape[0] // windows_block
    split_shape = (blocks, windows_block, WIN, heads_here, HEAD_DIM)
    score_scale = 1.0 / math.sqrt(HEAD_DIM)

    def one_block(carried, inputs):
        block_queries, block_keys, block_values, block_regions, block_totals, block_grad = inputs
        allowed = (block_regions[:, :, None] == block_regions[:, None, :])[:, None]
        scores = (
            jnp.einsum(
                "wihd,wjhd->whij", block_queries, block_keys, preferred_element_type=jnp.float32
            )
            * score_scale
        )
        logits = jnp.where(allowed, scores + bias_grid[None], masked_score)
        weights_soft = jnp.exp(logits - block_totals[..., None])
        soft_grad = jnp.einsum(
            "wihd,wjhd->whij", block_grad, block_values, preferred_element_type=jnp.float32
        )
        centre = jnp.sum(weights_soft * soft_grad, axis=3, keepdims=True)
        logit_grad = weights_soft * (soft_grad - centre)
        logit_grad_low = logit_grad.astype(jnp.bfloat16)
        query_grad = (
            jnp.einsum(
                "whij,wjhd->wihd", logit_grad_low, block_keys, preferred_element_type=jnp.float32
            )
            * score_scale
        )
        key_grad = (
            jnp.einsum(
                "whij,wihd->wjhd", logit_grad_low, block_queries, preferred_element_type=jnp.float32
            )
            * score_scale
        )
        value_grad = jnp.einsum(
            "whij,wihd->wjhd",
            weights_soft.astype(jnp.bfloat16),
            block_grad,
            preferred_element_type=jnp.float32,
        )
        return (carried + jnp.sum(logit_grad, axis=0), (query_grad, key_grad, value_grad))

    bias_grad, grads_out = lax.scan(
        one_block,
        jnp.zeros((heads_here, WIN, WIN), jnp.float32),
        (
            queries.reshape(split_shape),
            key_rows.reshape(split_shape),
            value_rows.reshape(split_shape),
            regions_here.reshape(blocks, windows_block, WIN),
            log_totals,
            attended_grad.reshape(split_shape),
        ),
    )
    flat_shape = queries.shape
    return (
        grads_out[0].reshape(flat_shape),
        grads_out[1].reshape(flat_shape),
        grads_out[2].reshape(flat_shape),
        bias_grad,
    )


def shards(
    tokens,
    regions,
    first_gain,
    first_shift,
    triple_weight,
    query_bias,
    value_bias,
    offset_table,
    output_weight,
    output_bias,
    second_gain,
    second_shift,
    inner_weight,
    inner_bias,
    outer_weight,
    outer_bias,
    cotangent,
):
    model_index = lax.axis_index("mp")
    model_count = lax.axis_size("mp")
    heads_part = offset_table.shape[0]
    inner_part = inner_weight.shape[1]
    fetched = (
        lax.all_gather(triple_weight.astype(jnp.bfloat16), "dp", axis=1, tiled=True),
        lax.all_gather(output_weight.astype(jnp.bfloat16), "dp", axis=1, tiled=True),
        lax.all_gather(inner_weight.astype(jnp.bfloat16), "dp", axis=0, tiled=True),
        lax.all_gather(outer_weight.astype(jnp.bfloat16), "dp", axis=1, tiled=True),
        lax.all_gather(first_gain.astype(jnp.bfloat16), "dp", axis=0, tiled=True),
        lax.all_gather(first_shift.astype(jnp.bfloat16), "dp", axis=0, tiled=True),
        lax.all_gather(query_bias.astype(jnp.bfloat16), "dp", axis=0, tiled=True),
        lax.all_gather(value_bias.astype(jnp.bfloat16), "dp", axis=0, tiled=True),
        lax.all_gather(output_bias.astype(jnp.bfloat16), "dp", axis=0, tiled=True),
        lax.all_gather(second_gain.astype(jnp.bfloat16), "dp", axis=0, tiled=True),
        lax.all_gather(second_shift.astype(jnp.bfloat16), "dp", axis=0, tiled=True),
        lax.all_gather(inner_bias.astype(jnp.bfloat16), "dp", axis=0, tiled=True),
        lax.all_gather(outer_bias.astype(jnp.bfloat16), "dp", axis=0, tiled=True),
    )
    first_gain_full = fetched[4].astype(jnp.float32)
    first_shift_full = fetched[5].astype(jnp.float32)
    query_full = fetched[6].astype(jnp.float32)
    value_full = fetched[7].astype(jnp.float32)
    output_bias_full = fetched[8].astype(jnp.float32)
    second_gain_full = fetched[9].astype(jnp.float32)
    second_shift_full = fetched[10].astype(jnp.float32)
    inner_bias_full = fetched[11].astype(jnp.float32)
    outer_bias_full = fetched[12].astype(jnp.float32)
    table_rounded = offset_table.astype(jnp.bfloat16)
    triple_here, output_here, inner_here, outer_here = (
        fetched[0],
        fetched[1],
        fetched[2],
        fetched[3],
    )
    table_here = table_rounded.astype(jnp.float32)
    head_first = model_index * heads_part
    inner_first = model_index * inner_part
    heads_here = table_here.shape[0]
    width_here = heads_here * HEAD_DIM
    query_here = lax.dynamic_slice_in_dim(query_full, head_first * HEAD_DIM, width_here)
    value_here = lax.dynamic_slice_in_dim(value_full, head_first * HEAD_DIM, width_here)
    inner_bias_here = lax.dynamic_slice_in_dim(inner_bias_full, inner_first, inner_here.shape[1])
    windows_block = max(1, WIN_BLOCK // heads_here)
    time_match, space_match = offset_matches()
    bias_grid = build_grid(table_here, time_match, space_match)
    tokens_float = tokens.astype(jnp.float32)
    normed_first, scaled_first, inverse_first = norm_forward(
        tokens_float, first_gain_full, first_shift_full
    )
    normed_first_low = normed_first.astype(jnp.bfloat16)
    first_rows = lax.all_gather(normed_first_low, "mp", axis=0, tiled=True)
    triple_cols = jnp.concatenate([triple_here[0], triple_here[1], triple_here[2]], axis=1)
    projected = product(first_rows, triple_cols)
    queries = (projected[:, :width_here] + query_here).astype(jnp.bfloat16)
    key_rows = projected[:, width_here : 2 * width_here].astype(jnp.bfloat16)
    value_rows = (projected[:, 2 * width_here :] + value_here).astype(jnp.bfloat16)
    attended_rows, log_totals, local_max = attend_forward(
        queries, key_rows, value_rows, regions, bias_grid, windows_block
    )
    attention_out = lax.psum_scatter(
        product(attended_rows, output_here).astype(jnp.bfloat16),
        "mp",
        scatter_dimension=0,
        tiled=True,
    ).astype(jnp.float32)
    middle = tokens_float + attention_out + output_bias_full
    normed_second, scaled_second, inverse_second = norm_forward(
        middle, second_gain_full, second_shift_full
    )
    normed_second_low = normed_second.astype(jnp.bfloat16)
    second_rows = lax.all_gather(normed_second_low, "mp", axis=0, tiled=True)
    before = product(second_rows, inner_here) + inner_bias_here
    hidden = jax.nn.gelu(before, approximate=False).astype(jnp.bfloat16)
    feed_out = lax.psum_scatter(
        product(hidden, outer_here).astype(jnp.bfloat16), "mp", scatter_dimension=0, tiled=True
    ).astype(jnp.float32)
    result = (middle + feed_out + outer_bias_full).astype(jnp.bfloat16)
    refetched = (
        lax.all_gather(triple_weight.astype(jnp.bfloat16), "dp", axis=1, tiled=True),
        lax.all_gather(output_weight.astype(jnp.bfloat16), "dp", axis=1, tiled=True),
        lax.all_gather(inner_weight.astype(jnp.bfloat16), "dp", axis=0, tiled=True),
        lax.all_gather(outer_weight.astype(jnp.bfloat16), "dp", axis=1, tiled=True),
    )
    triple_back, output_back, inner_back, outer_back = refetched
    upstream = cotangent.astype(jnp.float32)
    upstream_rows = lax.all_gather(cotangent, "mp", axis=0, tiled=True)
    hidden_grad = product_transposed(upstream_rows, outer_back)
    outer_grad = contract_rows(hidden, upstream_rows)
    before_grad = hidden_grad * gelu_slope(before)
    inner_bias_part = jnp.sum(before_grad, axis=0)
    before_grad_low = before_grad.astype(jnp.bfloat16)
    inner_grad = contract_rows(second_rows, before_grad_low)
    second_normed_grad = lax.psum_scatter(
        product_transposed(before_grad_low, inner_back).astype(jnp.bfloat16),
        "mp",
        scatter_dimension=0,
        tiled=True,
    ).astype(jnp.float32)
    middle_grad = upstream + norm_backward(
        second_normed_grad, scaled_second, inverse_second, second_gain_full
    )
    second_gain_part = jnp.sum(second_normed_grad * scaled_second, axis=0)
    second_shift_part = jnp.sum(second_normed_grad, axis=0)
    outer_bias_part = jnp.sum(upstream, axis=0)
    output_bias_part = jnp.sum(middle_grad, axis=0)
    middle_grad_low = middle_grad.astype(jnp.bfloat16)
    middle_rows = lax.all_gather(middle_grad_low, "mp", axis=0, tiled=True)
    attended_grad = product_transposed(middle_rows, output_back).astype(jnp.bfloat16)
    output_grad = contract_rows(attended_rows, middle_rows)
    query_grad, key_grad, value_grad, bias_grid_grad = attend_backward(
        queries, key_rows, value_rows, regions, bias_grid, log_totals, attended_grad, windows_block
    )
    query_bias_part = jnp.sum(query_grad, axis=0)
    value_bias_part = jnp.sum(value_grad, axis=0)
    triple_grad_rows = jnp.concatenate([query_grad, key_grad, value_grad], axis=1).astype(
        jnp.bfloat16
    )
    triple_flat = contract_rows(first_rows, triple_grad_rows)
    triple_grad = jnp.stack(
        [
            triple_flat[:, :width_here],
            triple_flat[:, width_here : 2 * width_here],
            triple_flat[:, 2 * width_here :],
        ]
    )
    triple_back_cols = jnp.concatenate([triple_back[0], triple_back[1], triple_back[2]], axis=1)
    first_normed_grad = lax.psum_scatter(
        product_transposed(triple_grad_rows, triple_back_cols).astype(jnp.bfloat16),
        "mp",
        scatter_dimension=0,
        tiled=True,
    ).astype(jnp.float32)
    token_grad = middle_grad + norm_backward(
        first_normed_grad, scaled_first, inverse_first, first_gain_full
    )
    first_gain_part = jnp.sum(first_normed_grad * scaled_first, axis=0)
    first_shift_part = jnp.sum(first_normed_grad, axis=0)
    table_grad = reduce_grid(bias_grid_grad, time_match, space_match)
    matrix_parts = (triple_grad, output_grad, inner_grad, outer_grad)
    summed = (
        lax.psum_scatter(
            matrix_parts[0].astype(jnp.bfloat16), "dp", scatter_dimension=1, tiled=True
        ).astype(jnp.float32),
        lax.psum_scatter(
            matrix_parts[1].astype(jnp.bfloat16), "dp", scatter_dimension=1, tiled=True
        ).astype(jnp.float32),
        lax.psum_scatter(
            matrix_parts[2].astype(jnp.bfloat16), "dp", scatter_dimension=0, tiled=True
        ).astype(jnp.float32),
        lax.psum_scatter(
            matrix_parts[3].astype(jnp.bfloat16), "dp", scatter_dimension=1, tiled=True
        ).astype(jnp.float32),
    )
    maxima_full = lax.dynamic_update_slice(
        jnp.full((HEADS,), masked_score, jnp.float32), local_max, (head_first,)
    )
    table_full = lax.dynamic_update_slice(
        jnp.zeros((HEADS, TABLE), jnp.float32), table_grad, (head_first, 0)
    )
    query_bias_full = lax.dynamic_update_slice(
        jnp.zeros((D,), jnp.float32), query_bias_part, (head_first * HEAD_DIM,)
    )
    value_bias_full = lax.dynamic_update_slice(
        jnp.zeros((D,), jnp.float32), value_bias_part, (head_first * HEAD_DIM,)
    )
    inner_bias_grad = lax.dynamic_update_slice(
        jnp.zeros((FF,), jnp.float32), inner_bias_part, (inner_first,)
    )

    def combine_stats(earlier, later):
        return (jnp.maximum(earlier[0], later[0]),) + tuple(
            (left_part + right_part for left_part, right_part in zip(earlier[1:], later[1:]))
        )

    merged = combined_all(
        (
            maxima_full,
            table_full,
            first_gain_part,
            first_shift_part,
            query_bias_full,
            value_bias_full,
            output_bias_part,
            second_gain_part,
            second_shift_part,
            inner_bias_grad,
            outer_bias_part,
        ),
        ("dp", "mp"),
        combine_stats,
    )
    flat_index = lax.axis_index("dp") * model_count + model_index
    device_count = lax.axis_size("dp") * model_count

    def own_piece(full_vector):
        width_piece = full_vector.shape[0] // device_count
        return lax.dynamic_slice_in_dim(full_vector, flat_index * width_piece, width_piece)

    own_first = model_index * heads_part
    my_maxima = lax.dynamic_slice_in_dim(merged[0], own_first, heads_part)
    my_table = lax.dynamic_slice_in_dim(merged[1], own_first, heads_part, 0)
    clip_factor = clip_target / jnp.maximum(my_maxima, clip_target)
    root_columns = jnp.repeat(jnp.sqrt(clip_factor), HEAD_DIM)
    clipped_weight = triple_weight[:2] * root_columns[None, None, :]
    return (
        result,
        token_grad.astype(jnp.bfloat16),
        own_piece(merged[2]),
        own_piece(merged[3]),
        summed[0],
        own_piece(merged[4]),
        own_piece(merged[5]),
        my_table,
        summed[1],
        own_piece(merged[6]),
        own_piece(merged[7]),
        own_piece(merged[8]),
        summed[2],
        own_piece(merged[9]),
        summed[3],
        own_piece(merged[10]),
        my_maxima,
        clipped_weight,
    )


def solution(mesh):
    placed = (
        P(("dp", "mp"), None),
        P("dp", None),
        P("dp"),
        P("dp"),
        P(None, "dp", "mp"),
        P("dp"),
        P("dp"),
        P("mp", None),
        P("mp", "dp"),
        P("dp"),
        P("dp"),
        P("dp"),
        P("dp", "mp"),
        P("dp"),
        P("mp", "dp"),
        P("dp"),
        P(("dp", "mp"), None),
    )
    return jax.shard_map(
        shards,
        mesh=mesh,
        in_specs=placed,
        out_specs=(
            P(("dp", "mp"), None),
            P(("dp", "mp"), None),
            P(("dp", "mp")),
            P(("dp", "mp")),
            P(None, "dp", "mp"),
            P(("dp", "mp")),
            P(("dp", "mp")),
            P("mp", None),
            P("mp", "dp"),
            P(("dp", "mp")),
            P(("dp", "mp")),
            P(("dp", "mp")),
            P("dp", "mp"),
            P(("dp", "mp")),
            P("mp", "dp"),
            P(("dp", "mp")),
            P("mp"),
            P(None, "dp", "mp"),
        ),
        check_vma=False,
    )
```

profile of v0, /device:TPU:0, one launch (start us, length us, event | category | flops | bytes accessed | tf_op | source)
XLA Modules:
  0.0 1625.6 jit_solution(13467831918895789429)
XLA Ops:
  16.3 23.9 %all-reduce.9 = (bf16[512]{0:T(512)(128)(2,1)S(1)}, bf16[512]{0:T(512)(128)(2,1)S(1)}, bf16[512]{0:T(512)(128)(2,1)S(1)}, bf16[512]{0:T(512)(128)(2,1)S(1)}, bf1...) all-reduce(bf16[512]{0:T(512)(128)(2,1)S(1)} %dynamic-update-slice., ...), channel_id=1, replica_groups=mesh['dp'=8,'mp'=4] {'dp'}, use_global_device_ids=true, to_apply=%add.6 | all-reduce | flops 4096 | bytes 16384
  67.6 30.5 %all_gather.121 = bf16[128,512]{0,1:T(8,128)(2,1)S(1)} all-gather(bf16[128,64]{0,1:T(8,128)(2,1)S(1)} %convert_element_type.461), channel_id=1, replica_groups=mesh['dp'=8,'mp'=4] {'dp'}, dimensions={1}, use_global_device_ids=true | all-gather | bytes 147456 | tf_op jit(solution)/shard_map/all_gather | solution.py:261
  98.1 31.2 %all_gather.118 = bf16[3,512,128]{2,1,0:T(8,128)(2,1)S(1)} all-gather(bf16[3,64,128]{2,1,0:T(8,128)(2,1)S(1)} %convert_element_type.453), channel_id=1, replica_groups=mesh['dp'=8,'mp'=4] {'dp'}, dimensions={1}, use_global_device_ids=true | all-gather | bytes 442368 | tf_op jit(solution)/shard_map/all_gather | solution.py:260
  170.9 128.9 %while.69 = (s32[]{:T(128)}, bf16[16,1,392,4,32]{2,4,3,1,0:T(8,128)(2,1)}, f32[16,1,4,392]{3,2,1,0:T(4,128)}, bf16[16,4]{1,0:T(8,128)(2,1)}, bf16[16,1,392,4,32]...) while((s32[]{:T(128)}, ...), condition=%wide.wide.region_6.7_spmd, body=%wide.wide.region_2.6_spmd.sunk | while | flops 85024800 | bytes 11477761 | solution.py:158
  312.7 56.4 %reduce-scatter.9.cloned.1.call-done = bf16[1568,512]{1,0:T(8,128)(2,1)} async-done(((bf16[6272,512]{1,0:T(8,128)(2,1)}), bf16[1568,512]{1,0:T(8,128)(2,1)}) %reduce-scatter.9.cloned.1.call-update) | async-done | bytes 1605648 | tf_op jit(solution)/shard_map/reduce_scatter | solution.py:315
  375.0 20.5 %all-gather.11 = bf16[8,1,256]{2,1,0:T(2,128)(2,1)S(1)} all-gather(bf16[1,1,256]{2,1,0:T(2,128)(2,1)S(1)} %reshape.626), channel_id=1, replica_groups=mesh['dp'=8,'mp'=4] {'dp'}, dimensions={0}, use_global_device_ids=true | all-gather | bytes 4608 | tf_op jit(solution)/shard_map/all_gather | solution.py:271
  395.6 33.4 %all_gather.128 = bf16[512,512]{0,1:T(8,128)(2,1)} all-gather(bf16[512,64]{0,1:T(8,128)(2,1)S(1)} %convert_element_type.475), channel_id=1, replica_groups=mesh['dp'=8,'mp'=4] {'dp'}, dimensions={1}, use_global_device_ids=true | all-gather | bytes 589824 | tf_op jit(solution)/shard_map/all_gather | solution.py:263
  429.0 33.3 %all_gather.126 = bf16[512,512]{1,0:T(8,128)(2,1)} all-gather(bf16[64,512]{1,0:T(8,128)(2,1)S(1)} %convert_element_type.471), channel_id=1, replica_groups=mesh['dp'=8,'mp'=4] {'dp'}, dimensions={0}, use_global_device_ids=true | all-gather | bytes 589824 | tf_op jit(solution)/shard_map/all_gather | solution.py:262
  462.3 33.8 %fusion.60 = (bf16[6272,512]{1,0:T(8,128)(2,1)}, f32[6272,512]{1,0:T(8,128)}) fusion(f32[512]{0:T(512)S(1)} %dynamic_slice.224, bf16[6272,512]{1,0:T(8,128)(2,1)} %all-gather.28.cloned.1.call-done, bf16[512,512]{1,0:T(8,128)(2,1)} %all_gather.126), kind=kOutput, calls=%fused_computation.85 | convolution fusion | flops 3500277760 | bytes 26216448 | tf_op jit(solution)/shard_map/dot_general | solution.py:60
  496.1 11.4 fusion.137
  515.7 10.2 convolution_convert_fusion.2
  526.5 44.8 %reduce-scatter.13.cloned.1.call-done = bf16[1568,512]{1,0:T(8,128)(2,1)} async-done(((bf16[6272,512]{1,0:T(8,128)(2,1)}), bf16[1568,512]{1,0:T(8,128)(2,1)}) %reduce-scatter.13.cloned.1.call-update) | async-done | bytes 1605648 | tf_op jit(solution)/shard_map/reduce_scatter | solution.py:348
  575.3 57.7 %reduce-scatter.11.cloned.1.call-done = bf16[1568,512]{1,0:T(8,128)(2,1)} async-done(((bf16[6272,512]{1,0:T(8,128)(2,1)}), bf16[1568,512]{1,0:T(8,128)(2,1)}) %reduce-scatter.11.cloned.1.call-update) | async-done | bytes 1605648 | tf_op jit(solution)/shard_map/reduce_scatter | solution.py:329
  641.5 9.1 convolution_convert_fusion.5
  657.5 9.1 fusion.112
  667.1 21.6 %all-gather.32.cloned.1.call-done = bf16[6272,512]{1,0:T(8,128)(2,1)} async-done(((bf16[1568,512]{1,0:T(8,128)(2,1)}), bf16[6272,512]{1,0:T(8,128)(2,1)}) %all-gather.32.cloned.1.call-update) | async-done | bytes 6422544 | tf_op jit(solution)/shard_map/all_gather | solution.py:362
  706.5 229.5 %while.70 = (s32[]{:T(128)}, f32[4,392,392]{1,2,0:T(8,128)}, f32[16,1,392,4,32]{2,4,3,1,0:T(8,128)}, bf16[16,1,392,4,32]{2,4,3,1,0:T(8,128)(2,1)}, f32[16,1,392,...) while((s32[]{:T(128)}, f32[4,392,392]{1,2,0:T(8,128)}, ...), condition=%wide.wide.region_16.17_spmd.clone, body=%wide.wide.region_14.16_spmd.clone.sunk | while | flops 204318240 | bytes 57371736 | solution.py:215
  936.0 9.1 fusion.135
  980.8 9.1 copy.112
  996.7 7.8 convolution_convert_fusion.6
  1012.2 7.9 convolution_convert_fusion
  1021.8 40.7 %all-gather.19 = bf16[32,1,512]{2,1,0:T(2,128)(2,1)S(1)} all-gather(bf16[1,1,512]{2,1,0:T(2,128)(2,1)S(1)} %reshape.642), channel_id=12, replica_groups=mesh['dp'=8,'mp'=4] {'dp','mp'}, dimensions={0}, use_global_device_ids=true | all-gather | bytes 33792 | tf_op jit(solution)/shard_map/all_gather | solution.py:30
  1063.7 37.0 %all-reduce.8 = bf16[512]{0:T(512)(128)(2,1)S(1)} all-reduce(bf16[512]{0:T(512)(128)(2,1)S(1)} %dynamic-update-slice.8), channel_id=2, replica_groups=mesh['dp'=8,'mp'=4] {'dp','mp'}, use_global_device_ids=true, to_apply=%add.8 | all-reduce | flops 512 | bytes 2048
  1102.0 40.8 %all-gather.9 = bf16[65536]{0:T(1024)(128)(2,1)S(1)} all-gather(bf16[2048]{0:T(1024)(128)(2,1)S(1)} %dynamic_update_slice.41), channel_id=11, replica_groups=mesh['dp'=8,'mp'=4] {'dp','mp'}, dimensions={0}, use_global_device_ids=true | all-gather | bytes 135168 | tf_op jit(solution)/shard_map/all_gather | solution.py:30
  1148.3 37.1 %all-gather.16 = bf16[32,1,512]{2,1,0:T(2,128)(2,1)S(1)} all-gather(bf16[1,1,512]{2,1,0:T(2,128)(2,1)S(1)} %reshape.636), channel_id=8, replica_groups=mesh['dp'=8,'mp'=4] {'dp','mp'}, dimensions={0}, use_global_device_ids=true | all-gather | bytes 33792 | tf_op jit(solution)/shard_map/all_gather | solution.py:30
  1186.0 38.5 %all-gather.17 = bf16[32,1,512]{2,1,0:T(2,128)(2,1)S(1)} all-gather(bf16[1,1,512]{2,1,0:T(2,128)(2,1)S(1)} %reshape.638), channel_id=9, replica_groups=mesh['dp'=8,'mp'=4] {'dp','mp'}, dimensions={0}, use_global_device_ids=true | all-gather | bytes 33792 | tf_op jit(solution)/shard_map/all_gather | solution.py:30
  1225.1 37.1 %all-gather.18 = bf16[32,1,512]{2,1,0:T(2,128)(2,1)S(1)} all-gather(bf16[1,1,512]{2,1,0:T(2,128)(2,1)S(1)} %reshape.640), channel_id=10, replica_groups=mesh['dp'=8,'mp'=4] {'dp','mp'}, dimensions={0}, use_global_device_ids=true | all-gather | bytes 33792 | tf_op jit(solution)/shard_map/all_gather | solution.py:30
  1263.5 38.0 %all-gather.15 = bf16[32,1,512]{2,1,0:T(2,128)(2,1)S(1)} all-gather(bf16[1,1,512]{2,1,0:T(2,128)(2,1)S(1)} %reshape.634), channel_id=7, replica_groups=mesh['dp'=8,'mp'=4] {'dp','mp'}, dimensions={0}, use_global_device_ids=true | all-gather | bytes 33792 | tf_op jit(solution)/shard_map/all_gather | solution.py:30
  1302.1 36.9 %all-gather.14 = bf16[32,1,512]{2,1,0:T(2,128)(2,1)S(1)} all-gather(bf16[1,1,512]{2,1,0:T(2,128)(2,1)S(1)} %reshape.632), channel_id=6, replica_groups=mesh['dp'=8,'mp'=4] {'dp','mp'}, dimensions={0}, use_global_device_ids=true | all-gather | bytes 33792 | tf_op jit(solution)/shard_map/all_gather | solution.py:30
  1347.1 38.0 %all-gather.12 = bf16[32,1,512]{2,1,0:T(2,128)(2,1)S(1)} all-gather(bf16[1,1,512]{2,1,0:T(2,128)(2,1)S(1)} %reshape.628), channel_id=4, replica_groups=mesh['dp'=8,'mp'=4] {'dp','mp'}, dimensions={0}, use_global_device_ids=true | all-gather | bytes 33792 | tf_op jit(solution)/shard_map/all_gather | solution.py:30
  1386.0 37.0 %all-gather.13 = bf16[32,1,512]{2,1,0:T(2,128)(2,1)S(1)} all-gather(bf16[1,1,512]{2,1,0:T(2,128)(2,1)S(1)} %reshape.630), channel_id=5, replica_groups=mesh['dp'=8,'mp'=4] {'dp','mp'}, dimensions={0}, use_global_device_ids=true | all-gather | bytes 33792 | tf_op jit(solution)/shard_map/all_gather | solution.py:30
  1423.7 183.4 %while.68 = (s32[]{:T(128)}, f32[16]{0:T(128)}, f32[16,2535]{1,0:T(8,128)S(1)}, f32[512]{0:T(512)S(1)}, f32[512]{0:T(512)S(1)}, /*index=5*/f32[512]{0:T(512)S(1)...) while((s32[]{:T(128)}, f32[16]{0:T(128)}, ...), condition=%wide.region_31.32_spmd, body=%wide.region_30.31_spmd.sunk | while | flops 93445 | bytes 516643 | solution.py:54
  (1146 shorter events, 765.2 us)
Async XLA Ops:
  7.2 37.6 %copy-start = (bf16[1568,512]{1,0:T(8,128)(2,1)S(1)}, bf16[1568,512]{1,0:T(8,128)(2,1)}, u32[]{:S(2)}) copy-start(bf16[1568,512]{1,0:T(8,128)(2,1)} %param.23) | copy-start | bytes 4816900
  7.2 122.2 %all-gather.26.cloned.1.call-start = ((), (), s32[]{:S(2)}) async-start(), calls=%async_computation.8 | async-start | bytes 8028160 | tf_op jit(solution)/shard_map/all_gather | solution.py:306
  46.7 322.4 %reduce-scatter.9.cloned.1.call-start = ((), (), s32[]{:S(2)}) async-start(), calls=%async_computation.9 | async-start | bytes 8028160 | tf_op jit(solution)/shard_map/reduce_scatter | solution.py:315
  98.1 209.8 %copy-start.12 = (bf16[128,512]{0,1:T(8,128)(2,1)}, bf16[128,512]{0,1:T(8,128)(2,1)S(1)}, u32[]{:S(2)}) copy-start(bf16[128,512]{0,1:T(8,128)(2,1)S(1)} %all_gather.121) | copy-start | bytes 393220
  299.8 8.2 copy-start.32
  312.6 56.5 %copy-start.1 = (bf16[1568,512]{1,0:T(8,128)(2,1)S(1)}, bf16[1568,512]{1,0:T(8,128)(2,1)}, u32[]{:S(2)}) copy-start(bf16[1568,512]{1,0:T(8,128)(2,1)} %param.23) | copy-start | bytes 4816900
  312.6 149.8 %all-gather.28.cloned.1.call-start = ((), (), s32[]{:S(2)}) async-start(), calls=%async_computation.10 | async-start | bytes 8028160 | tf_op jit(solution)/shard_map/all_gather | solution.py:326
  372.2 23.4 %copy-start.30 = (f32[64,512]{1,0:T(8,128)S(1)}, f32[64,512]{1,0:T(8,128)}, u32[]{:S(2)}) copy-start(f32[64,512]{1,0:T(8,128)} %param.35) | copy-start | bytes 393220
  372.2 23.4 %copy-start.31 = (f32[512,64]{0,1:T(8,128)S(1)}, f32[512,64]{0,1:T(8,128)}, u32[]{:S(2)}) copy-start(f32[512,64]{0,1:T(8,128)} %param.37) | copy-start | bytes 393220
  374.3 121.8 %all-gather.30.cloned.1.call-start = ((), (), s32[]{:S(2)}) async-start(), calls=%async_computation.12 | async-start | bytes 8028160 | tf_op jit(solution)/shard_map/all_gather | solution.py:341
  374.9 196.4 %reduce-scatter.13.cloned.1.call-start = ((), (), s32[]{:S(2)}) async-start(), calls=%async_computation.13 | async-start | bytes 8028160 | tf_op jit(solution)/shard_map/reduce_scatter | solution.py:348
  496.1 14.1 copy-start.20
  515.6 117.4 %reduce-scatter.11.cloned.1.call-start = ((), (), s32[]{:S(2)}) async-start(), calls=%async_computation.11 | async-start | bytes 8028160 | tf_op jit(solution)/shard_map/reduce_scatter | solution.py:329
  525.9 162.8 %all-gather.32.cloned.1.call-start = ((), (), s32[]{:S(2)}) async-start(), calls=%async_computation.14 | async-start | bytes 8028160 | tf_op jit(solution)/shard_map/all_gather | solution.py:362
  641.4 502.2 %reduce-scatter.23.cloned.1.call-start = ((), (), s32[]{:S(2)}) async-start(), calls=%async_computation.19 | async-start | bytes 589824 | tf_op jit(solution)/shard_map/reduce_scatter | solution.py:405
  650.6 494.5 %reduce-scatter.21.cloned.1.call-start = ((), (), s32[]{:S(2)}) async-start(), calls=%async_computation.18 | async-start | bytes 589824 | tf_op jit(solution)/shard_map/reduce_scatter | solution.py:402
  657.5 31.3 %copy-start.13 = (bf16[128,512]{0,1:T(8,128)(2,1)S(1)}, bf16[128,512]{0,1:T(8,128)(2,1)}, u32[]{:S(2)}) copy-start(bf16[128,512]{0,1:T(8,128)(2,1)} %copy-done.12) | copy-start | bytes 393220
  666.6 673.1 %reduce-scatter.19.cloned.1.call-start = ((), (), s32[]{:S(2)}) async-start(), calls=%async_computation.17 | async-start | bytes 147456 | tf_op jit(solution)/shard_map/reduce_scatter | solution.py:399
  936.0 9.1 copy-start.6
  936.0 9.1 copy-start.9
  992.6 348.4 %reduce-scatter.17.cloned.1.call-start = ((), (), s32[]{:S(2)}) async-start(), calls=%async_computation.16 | async-start | bytes 442368 | tf_op jit(solution)/shard_map/reduce_scatter | solution.py:396
  996.7 8.8 copy-start.35
  1005.4 6.7 copy-start.15
  1005.5 6.7 copy-start.17
  1005.5 337.0 %all-gather.34.cloned.1.call-start = ((), (), s32[]{:S(2)}) async-start(), calls=%async_computation.20 | async-start | bytes 2703360 | tf_op jit(solution)/shard_map/all_gather | solution.py:30
  1012.1 331.3 %reduce-scatter.15.cloned.1.call-start = ((), (), s32[]{:S(2)}) async-start(), calls=%async_computation.15 | async-start | bytes 8028160 | tf_op jit(solution)/shard_map/reduce_scatter | solution.py:382
  1020.1 43.1 %copy-start.40 = (bf16[16,4]{1,0:T(8,128)(2,1)S(1)}, bf16[16,4]{1,0:T(8,128)(2,1)}, u32[]{:S(2)}) copy-start(bf16[16,4]{1,0:T(8,128)(2,1)} %get-tuple-element.675) | copy-start | bytes 388
  1020.1 323.3 %copy-start.27 = (f32[1568]{0:T(1024)S(1)}, f32[1568]{0:T(1024)}, u32[]{:S(2)}) copy-start(f32[1568]{0:T(1024)} %copy-done.26) | copy-start | bytes 18820
  1020.1 323.3 %copy-start.29 = (f32[1568]{0:T(1024)S(1)}, f32[1568]{0:T(1024)}, u32[]{:S(2)}) copy-start(f32[1568]{0:T(1024)} %copy-done.28) | copy-start | bytes 18820
  1020.1 323.3 %copy-start.39 = (f32[512]{0:T(512)S(1)}, f32[512]{0:T(512)}, u32[]{:S(2)}) copy-start(f32[512]{0:T(512)} %copy-done.38) | copy-start | bytes 6148
  1343.4 42.3 %copy-start.10 = (bf16[1568,512]{1,0:T(8,128)(2,1)S(1)}, bf16[1568,512]{1,0:T(8,128)(2,1)}, u32[]{:S(2)}) copy-start(bf16[1568,512]{1,0:T(8,128)(2,1)} %reduce-scatter.15.cloned.1.call-done) | copy-start | bytes 4816900
  1347.1 266.6 %copy-start.23 = (f32[3,64,128]{2,1,0:T(8,128)S(1)}, f32[3,64,128]{2,1,0:T(8,128)}, u32[]{:S(2)}) copy-start(f32[3,64,128]{2,1,0:T(8,128)} %param.27) | copy-start | bytes 294916
  (70 other events, 279.7 us)
Sparse Core Ops, SparseCore 0:
  46.8 44.3 all-gather.25
  312.7 56.3 reduce-scatter.8
  374.4 47.1 all-gather.27
  423.1 47.1 all-gather.29
  515.7 55.5 reduce-scatter.12
  573.8 59.2 reduce-scatter.10
  641.6 47.1 all-gather.31
  692.4 61.8 reduce-scatter.22
  757.7 61.0 reduce-scatter.20
  992.8 60.9 reduce-scatter.18
  1057.9 61.0 reduce-scatter.16
  1122.2 57.0 all-gather.33
  1182.0 58.7 reduce-scatter.14
where the time goes:
time: 1650 us; the launch traced here: 1630 us
  blocking collectives  554 us (34%)
  matrix products  380 us (23%)
  other arithmetic  293 us (18%)
  local copies, waits for them, and re-layouts  198 us (12%)
  waiting for transfers between devices  181 us (11%)
    all_gather x9, blocking collectives, combined_all(): lax.all_gather(a.astype(kind), axis)  344 us
    convert_element_type x166, other arithmetic, take(): lax.dynamic_index_in_dim(a, source, 0, False).astype(own.dtype)  115 us
    dot_general x32, matrix products, one_block(): jnp.einsum('wihd,wjhd->whij', block_queries, block_keys, preferred_elemen...  90.6 us
    unnamed x2, blocking collectives  60.9 us
    reduce_scatter x1, waiting for transfers between devices, shards(): lax.psum_scatter(product(hidden, outer_here).astype(jnp.bfloat16), 'mp',...  57.7 us
    reduce_scatter x1, waiting for transfers between devices, shards(): lax.psum_scatter(product(attended_rows, output_here).astype(jnp.bfloat16)...  56.4 us
    dot_general x4, matrix products, product(): return jnp.dot(left, right, preferred_element_type=jnp.float32)  54.2 us
    reduce_scatter x1, waiting for transfers between devices, shards(): lax.psum_scatter(product_transposed(before_grad_low, inner_back).astype(j...  44.8 us
  transfers between devices with their start and end apart: 13, of which 4 were waited for; matrix products, arithmetic and copies ran while one was open for 27% of the time, Pallas kernels for 0%

commit v1 on v0

v1 whole, which is shorter than its diff:
```python
import math, functools
import numpy as np
import jax, jax.numpy as jnp
from jax import lax
from jax.experimental import pallas as pl
from jax.experimental.pallas import tpu as pltpu
from jax.sharding import PartitionSpec as P

D = 512
HEADS = 16
HEAD_DIM = 32
FF = 2048
WIN = 392
PLACES = 49
TIMES = 8
SPACE = 169
TABLE = 2535
GROUP = 128
norm_epsilon = 1e-05
masked_score = -1e9
clip_target = 10.0
log2e = math.log2(math.e)
score_scale = 1.0 / math.sqrt(HEAD_DIM)
bf = jnp.bfloat16
f32 = jnp.float32
ROWS = [(s, min(64, WIN - s)) for s in range(0, WIN, 64)]


def dd(a, b, ca, cb):
    return lax.dot_general(a, b, (((ca,), (cb,)), ((), ())), preferred_element_type=f32)


def fold_max(acc, x):
    for r in range(0, x.shape[0], 8):
        acc = jnp.maximum(acc, x[r:r + 8])
    return acc


def load_blocks(me, blocks, src, dst, sem, rows):
    copies = []
    for k, blk in enumerate(blocks):
        at = pl.multiple_of((me ^ blk) * rows, rows)
        copies.append(pltpu.make_async_copy(src.at[k], dst.at[pl.ds(at, rows)], sem.at[k]))
        copies[-1].start()
    for c in copies:
        c.wait()


def fwd_kernel(first, blocks, *refs):
    if first:
        (me_ref, x_ref, ln_ref, w_hbm, qv_ref, t2_ref, rr_ref, rc_ref,
         n1_out, qkv_out, e_out, ot_out, o_out, linv_out, hm_out, w_out,
         wscr, bias, mask, s_scr, wsem) = refs
    else:
        (me_ref, n1_ref, w_hbm, qv_ref, t2_ref, rr_ref, rc_ref,
         qkv_out, e_out, ot_out, o_out, linv_out, hm_out, w_out,
         wscr, bias, mask, s_scr, wsem) = refs
    w = pl.program_id(0)

    @pl.when(w == 0)
    def _():
        load_blocks(me_ref[0], blocks, w_hbm, wscr, wsem, w_hbm.shape[1])
        w_out[...] = wscr[...]
        for h in range(4):
            for t in range(TIMES):
                bias[h, t * PLACES:(t + 1) * PLACES, :] = t2_ref[h, 0:PLACES, (7 - t) * PLACES:(7 - t) * PLACES + WIN]
        hm_out[...] = jnp.full(hm_out.shape, -jnp.inf, f32)

    mask[...] = jnp.where(rc_ref[0] == rr_ref[0], 0.0, masked_score)
    if first:
        x = x_ref[0].astype(f32)
        xc = x - jnp.mean(x, axis=1, keepdims=True)
        inv = lax.rsqrt(jnp.mean(xc * xc, axis=1, keepdims=True) + norm_epsilon)
        n1 = (xc * inv * ln_ref[0:1] + ln_ref[1:2]).astype(bf)
        n1_out[0] = n1
    else:
        n1 = n1_ref[0]
    p = dd(n1, wscr[...], 1, 0)
    q = (p[:, :128] + qv_ref[0:1]) * (score_scale * log2e)
    kb = p[:, 128:256].astype(bf)
    v = p[:, 256:] + qv_ref[1:2]
    qkv_out[0, :, 0:128] = q.astype(bf)
    qkv_out[0, :, 128:256] = kb
    qkv_out[0, :, 256:384] = v.astype(bf)
    qT = q.T.astype(bf)
    vT = v.T.astype(bf)
    ones = jnp.ones((16, WIN), bf)
    outs, linvs = [], []
    for h in range(4):
        sl = slice(h * 32, h * 32 + 32)
        s_scr[...] = dd(kb[:, sl], qT[sl], 1, 0)
        hm = jnp.full((8, WIN), -jnp.inf, f32)
        m = jnp.full((8, WIN), -jnp.inf, f32)
        for r, n in ROWS:
            c = s_scr[r:r + n]
            hm = fold_max(hm, c)
            c = c + bias[h, r:r + n] + mask[r:r + n]
            m = fold_max(m, c)
            s_scr[r:r + n] = c
        hm_out[h] = jnp.maximum(hm_out[h], hm)
        m = jnp.max(m, axis=0, keepdims=True)
        for r, n in ROWS:
            e_out[0, h, r:r + n] = jnp.exp2(s_scr[r:r + n] - m).astype(bf)
        ol = dd(jnp.concatenate([vT[sl], ones], axis=0), e_out[0, h], 1, 0)
        linv = 1.0 / ol[32:33]
        linvs.append(linv)
        outs.append(ol[:32] * linv)
    oT = jnp.concatenate(outs, axis=0)
    ot_out[0] = oT.astype(bf)
    o_out[0] = oT.T.astype(bf)
    linv_out[0] = jnp.concatenate(linvs + [jnp.zeros((4, WIN), f32)], axis=0)


def full(shape):
    return pl.BlockSpec(shape, lambda w, me: (0,) * len(shape))


def win(shape):
    return pl.BlockSpec((1,) + shape, lambda w, me: (w,) + (0,) * len(shape))


def attend_fwd(first, me, x, ln, wblk, qv, t2, rr, rc, blocks):
    nw = x.shape[0]
    sds = jax.ShapeDtypeStruct
    ins = [x] + ([ln] if first else []) + [wblk, qv, t2, rr, rc]
    in_specs = ([win((WIN, D))] + ([full(ln.shape)] if first else []) +
                [pl.BlockSpec(memory_space=pl.ANY), full(qv.shape), full(t2.shape), win((1, WIN)), win((WIN, 1))])
    outs = ([sds((nw, WIN, D), bf)] if first else []) + [
        sds((nw, WIN, 384), bf), sds((nw, 4, WIN, WIN), bf), sds((nw, GROUP, WIN), bf), sds((nw, WIN, GROUP), bf),
        sds((nw, 8, WIN), f32), sds((4, 8, WIN), f32), sds((D, 384), bf)]
    out_specs = ([win((WIN, D))] if first else []) + [
        win((WIN, 384)), win((4, WIN, WIN)), win((GROUP, WIN)), win((WIN, GROUP)), win((8, WIN)), full((4, 8, WIN)), full((D, 384))]
    return pl.pallas_call(
        functools.partial(fwd_kernel, first, blocks), out_shape=outs,
        grid_spec=pltpu.PrefetchScalarGridSpec(
            num_scalar_prefetch=1, grid=(nw,), in_specs=in_specs, out_specs=out_specs,
            scratch_shapes=[pltpu.VMEM((D, 384), bf), pltpu.VMEM((4, WIN, WIN), f32), pltpu.VMEM((WIN, WIN), f32),
                            pltpu.VMEM((WIN, WIN), f32), pltpu.SemaphoreType.DMA((wblk.shape[0],))]),
        compiler_params=pltpu.CompilerParams(vmem_limit_bytes=48 * 2**20),
        cost_estimate=pl.CostEstimate(flops=nw * 2 * 10**9, bytes_accessed=nw * 4 * 10**6, transcendentals=nw * 4 * WIN * WIN),
    )(me, *ins)


def bwd_kernel(first, last, blocks, *refs):
    refs = list(refs)
    take = lambda n: [refs.pop(0) for _ in range(n)]
    me_ref, n1_ref, qkv_ref, e_ref, ot_ref, linv_ref, dyb_ref, wo_ref, w_ref = take(9)
    prev_ref = None if first else take(1)[0]
    if last:
        x_ref, dy_ref, ln_ref = take(3)
    dn_out, dw_out, t2_out, vec_out = take(4)
    if last:
        ln_out, = take(1)
    dwacc, dls, p_scr, dl_scr = take(4)
    w = pl.program_id(0)

    @pl.when(w == 0)
    def _():
        dwacc[...] = jnp.zeros(dwacc.shape, f32)
        dls[...] = jnp.zeros(dls.shape, f32)
        vec_out[...] = jnp.zeros(vec_out.shape, f32)
        if last:
            ln_out[...] = jnp.zeros(ln_out.shape, f32)

    q = qkv_ref[0, :, 0:128]
    k = qkv_ref[0, :, 128:256]
    v = qkv_ref[0, :, 256:384]
    do = dd(dyb_ref[0], wo_ref[...], 1, 0)
    doT = do.T
    oT = ot_ref[0].astype(f32)
    scaled = []
    rs = []
    for h in range(4):
        sl = slice(h * 32, h * 32 + 32)
        s = (doT[sl] * linv_ref[0, h:h + 1]).astype(bf)
        scaled.append(s)
        rs.append(jnp.sum(s.astype(f32) * oT[sl], axis=0, keepdims=True))
    doTs = jnp.concatenate(scaled, axis=0)
    dos = doTs.astype(f32).T.astype(bf)
    kT = k.astype(f32).T.astype(bf)
    lane = lax.broadcasted_iota(jnp.int32, (1, 128), 1) // 32
    dk = jnp.zeros((WIN, 128), f32)
    dv = jnp.zeros((WIN, 128), f32)
    dqT = []
    for h in range(4):
        sl = slice(h * 32, h * 32 + 32)
        p_scr[...] = dd(v[:, sl], doTs[sl], 1, 0)
        for r, n in ROWS:
            dl = e_ref[0, h, r:r + n].astype(f32) * (p_scr[r:r + n] - rs[h])
            dls[h, r:r + n] += dl
            dl_scr[r:r + n] = dl.astype(bf)
        dqT.append(dd(kT[sl], dl_scr[...], 1, 0))
        own = lane == h
        dk += dd(dl_scr[...], jnp.where(own, q, jnp.zeros((), bf)), 1, 0)
        dv += dd(e_ref[0, h], jnp.where(own, dos, jnp.zeros((), bf)), 1, 0)
    dq = jnp.concatenate(dqT, axis=0).T * score_scale
    dk = dk * (1.0 / log2e)
    vec_out[0:1] += jnp.sum(dq, axis=0, keepdims=True)
    vec_out[1:2] += jnp.sum(dv, axis=0, keepdims=True)
    dqkv = jnp.concatenate([dq.astype(bf), dk.astype(bf), dv.astype(bf)], axis=1)
    dwacc[...] += dd(n1_ref[0], dqkv, 0, 0)
    dn1 = dd(dqkv, w_ref[...], 1, 1)
    if not first:
        dn1 = dn1 + prev_ref[0]
    if last:
        x = x_ref[0].astype(f32)
        xc = x - jnp.mean(x, axis=1, keepdims=True)
        inv = lax.rsqrt(jnp.mean(xc * xc, axis=1, keepdims=True) + norm_epsilon)
        u = xc * inv
        ln_out[0:1] += jnp.sum(dn1 * u, axis=0, keepdims=True)
        ln_out[1:2] += jnp.sum(dn1, axis=0, keepdims=True)
        a = dn1 * ln_ref[0:1]
        g = inv * (a - jnp.mean(a, axis=1, keepdims=True) - u * jnp.mean(a * u, axis=1, keepdims=True))
        dn_out[0] = (dy_ref[0] + g).astype(bf)
    else:
        dn_out[0] = dn1

    @pl.when(w == pl.num_programs(0) - 1)
    def _():
        rows = dw_out.shape[1]
        for kk, blk in enumerate(blocks):
            at = pl.multiple_of((me_ref[0] ^ blk) * rows, rows)
            dw_out[kk] = dwacc[pl.ds(at, rows), :].astype(bf)
        t2_out[...] = jnp.zeros(t2_out.shape, f32)
        for h in range(4):
            for t in range(TIMES):
                lo = (7 - t) * PLACES
                t2_out[h, 0:PLACES, lo:lo + WIN] += dls[h, t * PLACES:(t + 1) * PLACES, :]


def attend_bwd(me, n1, qkv, e, oT, linv, dyb, wo, w, prev, last, blocks):
    nblk = len(blocks)
    nw = n1.shape[0]
    sds = jax.ShapeDtypeStruct
    first = prev is None
    ins = [n1, qkv, e, oT, linv, dyb, wo, w] + ([] if first else [prev]) + (list(last) if last else [])
    in_specs = ([win((WIN, D)), win((WIN, 384)), win((4, WIN, WIN)), win((GROUP, WIN)), win((8, WIN)), win((WIN, D)),
                 full((D, GROUP)), full((D, 384))] + ([] if first else [win((WIN, D))]) +
                ([win((WIN, D)), win((WIN, D)), full(last[2].shape)] if last else []))
    outs = [sds((nw, WIN, D), bf if last else f32), sds((nblk, D // nblk, 384), bf), sds((4, 56, 768), f32), sds((8, 128), f32)]
    out_specs = [win((WIN, D)), full((nblk, D // nblk, 384)), full((4, 56, 768)), full((8, 128))]
    if last:
        outs.append(sds((8, D), f32))
        out_specs.append(full((8, D)))
    return pl.pallas_call(
        functools.partial(bwd_kernel, first, bool(last), blocks), out_shape=outs,
        grid_spec=pltpu.PrefetchScalarGridSpec(
            num_scalar_prefetch=1, grid=(nw,), in_specs=in_specs, out_specs=out_specs,
            scratch_shapes=[pltpu.VMEM((D, 384), f32), pltpu.VMEM((4, WIN, WIN), f32), pltpu.VMEM((WIN, WIN), f32),
                            pltpu.VMEM((WIN, WIN), bf)]),
        compiler_params=pltpu.CompilerParams(vmem_limit_bytes=48 * 2**20),
        cost_estimate=pl.CostEstimate(flops=nw * 4 * 10**9, bytes_accessed=nw * 5 * 10**6, transcendentals=0),
    )(me, *ins)


def mlp_kernel(na, *refs):
    places, nblk, brow = na
    refs = list(refs)
    take = lambda n: [refs.pop(0) for _ in range(n)]
    narr = 1 + max(p[0] for p in places)
    me_ref, x_ref, g_ref = take(3)
    o_refs = take(4)
    vin_ref, bi_ref = take(2)
    w_hbm = take(narr)
    res_out, dy_out, dyb_out, wo_out, vec_out, dbi_out = take(6)
    g_outs = take(narr)
    wscr, acc, wsem = take(3)
    t = pl.program_id(0)
    me = me_ref[0]

    @pl.when(t == 0)
    def _():
        copies = []
        for i, (arr, idx, k, blk, off) in enumerate(places):
            at = pl.multiple_of((me ^ blk) * (D // nblk) + off, brow)
            copies.append(pltpu.make_async_copy(w_hbm[arr].at[idx], wscr.at[k, pl.ds(at, brow)], wsem.at[i]))
            copies[-1].start()
        acc[...] = jnp.zeros(acc.shape, f32)
        vec_out[...] = jnp.zeros(vec_out.shape, f32)
        dbi_out[...] = jnp.zeros(dbi_out.shape, f32)
        for c in copies:
            c.wait()

    o = jnp.concatenate([r[...] for r in o_refs], axis=1)
    y = x_ref[...].astype(f32) + vin_ref[0:1]
    for k in range(4):
        y = y + dd(o_refs[k][...], wscr[k, :, 0:128], 1, 1)
    yc = y - jnp.mean(y, axis=1, keepdims=True)
    inv = lax.rsqrt(jnp.mean(yc * yc, axis=1, keepdims=True) + norm_epsilon)
    u = yc * inv
    n2 = (u * vin_ref[1:2] + vin_ref[2:3]).astype(bf)
    gb = g_ref[...]
    gT = gb.astype(f32).T.astype(bf)
    n2T = n2.astype(f32).T.astype(bf)
    ff = jnp.zeros(y.shape, f32)
    dn2 = jnp.zeros(y.shape, f32)
    for k in range(4):
        wi = wscr[k, :, 128:640]
        wo = wscr[k, :, 640:1152]
        z = dd(n2, wi, 1, 0) + bi_ref[:, k * 512:(k + 1) * 512]
        ez = jnp.exp2(z * z * (-0.5 * log2e))
        tt = 1.0 / (1.0 + (0.3275911 * 0.7071067811865476) * jnp.abs(z))
        poly = tt * (0.254829592 + tt * (-0.284496736 + tt * (1.421413741 + tt * (-1.453152027 + tt * 1.061405429))))
        tail = 0.5 * poly * ez
        phi = jnp.where(z >= 0, 1.0 - tail, tail)
        hb = (z * phi).astype(bf)
        slope = phi + z * (ez * 0.3989422804014327)
        ff = ff + dd(hb, wo, 1, 1)
        dz = dd(gb, wo, 1, 0) * slope
        dbi_out[0:1, k * 512:(k + 1) * 512] += jnp.sum(dz, axis=0, keepdims=True)
        dzb = dz.astype(bf)
        dn2 = dn2 + dd(dzb, wi, 1, 1)
        acc[k, :, 640:1152] += dd(gT, hb, 1, 0)
        acc[k, :, 128:640] += dd(n2T, dzb, 1, 0)
    res_out[...] = (y + ff + vin_ref[3:4]).astype(bf)
    g = gb.astype(f32)
    a = dn2 * vin_ref[1:2]
    dy = g + inv * (a - jnp.mean(a, axis=1, keepdims=True) - u * jnp.mean(a * u, axis=1, keepdims=True))
    dy_out[...] = dy
    dyb = dy.astype(bf)
    dyb_out[...] = dyb
    dyT = dy.T.astype(bf)
    for k in range(4):
        acc[k, :, 0:128] += dd(dyT, o_refs[k][...], 1, 0)
    vec_out[0:1] += jnp.sum(g, axis=0, keepdims=True)
    vec_out[1:2] += jnp.sum(dn2 * u, axis=0, keepdims=True)
    vec_out[2:3] += jnp.sum(dn2, axis=0, keepdims=True)
    vec_out[3:4] += jnp.sum(dy, axis=0, keepdims=True)

    @pl.when(t == pl.num_programs(0) - 1)
    def _():
        wo_out[...] = wscr[:, :, 0:128]
        for arr, idx, k, blk, off in places:
            at = pl.multiple_of((me ^ blk) * (D // nblk) + off, brow)
            g_outs[arr][idx] = acc[k, pl.ds(at, brow), :].astype(bf)


def mlp(me, x, g, o_list, vin, bi, warrs, places, nblk, tile):
    T = x.shape[0]
    sds = jax.ShapeDtypeStruct
    brow = warrs[0].shape[1]
    row = lambda c: pl.BlockSpec((tile, c), lambda i, me: (i, 0))
    one = lambda s: pl.BlockSpec(s, lambda i, me: (0,) * len(s), pipeline_mode=pl.Buffered(1))
    ins = [x, g] + list(o_list) + [vin, bi] + list(warrs)
    in_specs = [row(D), row(D)] + [row(GROUP)] * 4 + [one(vin.shape), one(bi.shape)] + [pl.BlockSpec(memory_space=pl.ANY)] * len(warrs)
    outs = [sds((T, D), bf), sds((T, D), f32), sds((T, D), bf), sds((4, D, GROUP), bf), sds((8, D), f32), sds((8, FF), f32)]
    out_specs = [row(D), row(D), row(D), one((4, D, GROUP)), one((8, D)), one((8, FF))]
    for wa in warrs:
        outs.append(sds(wa.shape, bf))
        out_specs.append(one(wa.shape))
    return pl.pallas_call(
        functools.partial(mlp_kernel, (places, nblk, brow)), out_shape=outs,
        grid_spec=pltpu.PrefetchScalarGridSpec(
            num_scalar_prefetch=1, grid=(T // tile,), in_specs=in_specs, out_specs=out_specs,
            scratch_shapes=[pltpu.VMEM((4, D, 1152), bf), pltpu.VMEM((4, D, 1152), f32), pltpu.SemaphoreType.DMA((len(places),))]),
        compiler_params=pltpu.CompilerParams(vmem_limit_bytes=56 * 2**20),
        cost_estimate=pl.CostEstimate(flops=T * 16 * 10**6, bytes_accessed=30 * 10**6, transcendentals=T * FF * 2),
    )(me, *ins)


def place_onehot():
    at = np.arange(PLACES)
    code = (at // 7) * 13 + at % 7
    off = code[None, :] - code[:, None] + 84
    return (off.reshape(-1)[None, :] == np.arange(SPACE)[:, None]).astype(np.float32)


def spread_table(table):
    n = table.shape[0]
    t = jnp.dot(table.astype(bf).reshape(n * 15, SPACE), jnp.asarray(place_onehot(), bf), preferred_element_type=f32)
    t = t.reshape(n, 15, PLACES, PLACES).transpose(0, 2, 1, 3).reshape(n, PLACES, 15 * PLACES) * log2e
    return jnp.pad(t, ((0, 0), (0, 56 - PLACES), (0, 768 - 15 * PLACES)))


def fold_table(t2):
    n = t2.shape[0]
    t = t2[:, :PLACES, :15 * PLACES].reshape(n, PLACES, 15, PLACES).transpose(0, 2, 1, 3).reshape(n * 15, PLACES * PLACES)
    return lax.dot_general(t, jnp.asarray(place_onehot()), (((1,), (1,)), ((), ())), preferred_element_type=f32).reshape(n, TABLE)


def swap(x, axis, bit):
    return lax.ppermute(x, axis, [(i, i ^ bit) for i in range(lax.axis_size(axis))])


def xor_onehot(me, n):
    at = jnp.arange(n)
    return ((at[:, None] ^ at[None, :]) == me)


def xor_order(x, me):
    hot = xor_onehot(me, x.shape[0]).astype(f32)
    return jnp.sum(hot.reshape(hot.shape + (1,) * (x.ndim - 1)) * x[None], axis=1)


Z1, Z0, Y, X, C = ("dp", 4), ("dp", 2), ("dp", 1), ("mp", 2), ("mp", 1)
DP_BLOCKS = [(p & 1) * 4 + (p & 2) + (p >> 2) for p in range(8)]
ORDER_A = [Z1, Z0, Y, X]
ORDER_B = [Z1, Z0, X, Y]


def rest_places():
    out = []
    for arr in range(4):
        for i in range(16):
            first, second = i >> 3, (i >> 2) & 1
            x, y = (first, second) if arr < 2 else (second, first)
            out.append((arr, i, (arr % 2) + 2 * x, (i & 1) * 4 + (i & 2) + y, 32 * (arr // 2)))
    return out


def gather(x, order):
    for axis, bit in order:
        x = jnp.concatenate([x, swap(x, axis, bit)], axis=0)
    return x


def scatter(g, order):
    for axis, bit in order[::-1]:
        half = g.shape[0] // 2
        g = g[:half] + swap(g[half:], axis, bit)
    return g


def canonical(a, parts):
    m, d, rows, width = a.shape
    own = width // parts
    a = a.reshape(4, m // 4, d, rows, parts, own).transpose(0, 2, 3, 4, 1, 5)
    return a.reshape(4, d * rows, parts * (m // 4) * own)


def uncanonical(a, parts, m, d):
    own = a.shape[2] // parts // (m // 4)
    a = a.reshape(4, d, D // d, parts, m // 4, own).transpose(0, 4, 1, 2, 3, 5)
    return a.reshape(m, d, D // d, parts * own)


def shards(tokens, regions, first_gain, first_shift, triple_weight, query_bias, value_bias, offset_table, output_weight,
           output_bias, second_gain, second_shift, inner_weight, inner_bias, outer_weight, outer_bias, cotangent):
    ndp, nmp = lax.axis_size("dp"), lax.axis_size("mp")
    me_dp, me_mp = lax.axis_index("dp"), lax.axis_index("mp")
    fast = (ndp, nmp) == (8, 4)
    T = tokens.shape[0]
    nw = T // WIN
    rows, own = D // ndp, D // nmp
    both = ("mp", "dp")

    triple_local = triple_weight.transpose(1, 0, 2).reshape(rows, 3 * own).astype(bf)
    rest_local = [output_weight.T.astype(bf), inner_weight.astype(bf), outer_weight.T.astype(bf)]
    small = jnp.concatenate([first_gain, first_shift, query_bias, value_bias, output_bias, second_gain, second_shift,
                             outer_bias, inner_bias]).astype(bf)
    if fast:
        me = me_dp.astype(jnp.int32).reshape(1)
        group_me = me_mp
        pad = jnp.pad(small, (0, 16 * 384 - small.shape[0])).reshape(16, 384)
        packed = gather(jnp.concatenate([triple_local, pad], axis=0)[None], [Z1, Z0, Y])
        hot = xor_onehot(me_dp, 8)[:, np.array(DP_BLOCKS)].astype(bf)
        small_all = jnp.dot(hot, packed[:, 64:66].reshape(8, 768), preferred_element_type=f32)
        w0 = packed[:, :64]
        w1 = swap(w0, *C)
        w2 = swap(w0, *X)
        w3 = swap(w2, *C)
        wblocks = [w0, w1, w2, w3]
        blocks = DP_BLOCKS
        t0 = offset_table.astype(bf)
        t01 = jnp.concatenate([t0, swap(t0, *C)], axis=0)
        tables = jnp.concatenate([t01, swap(t01, *X)], axis=0)
        rest = jnp.concatenate(rest_local, axis=1)
        ra = gather(rest[None, :32], ORDER_A)
        rb = gather(rest[None, 32:], ORDER_B)
        warrs = [ra, swap(ra, *C), rb, swap(rb, *C)]
        places = rest_places()
    else:
        me = jnp.zeros((1,), jnp.int32)
        group_me = jnp.int32(0)
        small_all = lax.all_gather(small, "dp").astype(f32)
        shape = (nmp, ndp, rows, -1)
        wcanon = canonical(lax.all_gather(triple_local, both).reshape(shape), 3)
        wblocks = [wcanon[k:k + 1] for k in range(4)]
        blocks = [0]
        tables = lax.all_gather(offset_table.astype(bf), "mp", tiled=True)
        warrs = [jnp.concatenate([canonical(lax.all_gather(r, both).reshape(shape), 1) for r in rest_local], axis=2)]
        places = [(0, k, k, 0, 0) for k in range(4)]
    nblk = len(blocks)
    eight = small_all[:, :8 * rows].reshape(ndp, 8, rows).transpose(1, 0, 2).reshape(8, D)
    bi = xor_order(small_all[:, 8 * rows:].reshape(4, 512), group_me).reshape(1, FF)
    ln1 = jnp.pad(eight[0:2], ((0, 6), (0, 0)))
    qv = xor_order(eight[2:4].reshape(2, 4, GROUP).transpose(1, 0, 2), group_me)
    qv = jnp.pad(qv, ((0, 0), (0, 6), (0, 0)))
    vin = jnp.pad(eight[4:8], ((0, 4), (0, 0)))
    t2 = spread_table(tables)

    mine = lax.dynamic_slice_in_dim(regions, me_mp * nw, nw)
    rr, rc = mine[:, None, :], mine[:, :, None]
    x3 = tokens.reshape(nw, WIN, D)
    saved = []
    for k in range(4):
        t2k = t2[4 * k:4 * k + 4]
        if k == 0:
            n1, *kept = attend_fwd(True, me, x3, ln1, wblocks[k], qv[k], t2k, rr, rc, blocks)
        else:
            kept = attend_fwd(False, me, n1, None, wblocks[k], qv[k], t2k, rr, rc, blocks)
        saved.append(kept)
    tile = 392 if T % 392 == 0 else T
    flat = lambda a: a.reshape(T, a.shape[-1])
    result, dy, dyb, wo, vec, dbi, *rest_grads = mlp(
        me, tokens, cotangent, [flat(s[3]) for s in saved], vin, bi, warrs, places, nblk, tile)
    peaks = jnp.stack([jnp.max(s[5], axis=(1, 2)) for s in saved]) * (1.0 / log2e)
    peaks = xor_order(peaks, group_me).reshape(1, HEADS)

    grads = {}
    dn = None
    for k in (3, 2, 1, 0):
        qkv, e, ot, _, linv, _, w = saved[k]
        last = (x3, dy.reshape(nw, WIN, D), ln1) if k == 0 else None
        out = attend_bwd(me, n1, qkv, e, ot, linv, dyb.reshape(nw, WIN, D), wo[k], w, dn, last, blocks)
        dn = out[0]
        grads[k] = out[1:]
    dx = dn.reshape(T, D)
    lnvec = grads[0][3]

    sums1 = jnp.concatenate([vec[0:4].reshape(-1), xor_order(dbi[0].reshape(4, 512), group_me).reshape(-1)])
    table_grads = [fold_table(grads[k][1]) for k in range(4)]
    qvg = xor_order(jnp.stack([grads[k][2][0:2] for k in range(4)]), group_me)
    sums2 = jnp.concatenate([lnvec[0:2].reshape(-1), qvg.transpose(1, 0, 2).reshape(-1)])
    if fast:
        v = jnp.concatenate([sums1, jnp.pad(peaks[0], (0, 128 - HEADS))]).reshape(33, 128)
        top = lax.broadcasted_iota(jnp.int32, (33, 128), 0) == 32
        for axis, bit in (C, X, Y, Z0, Z1):
            r = swap(v, axis, bit)
            v = jnp.where(top, jnp.maximum(v, r), v + r)
        sums1 = v[:32].reshape(-1)
        peaks = v[32, :HEADS]
        ka, sa, kb, sb = rest_grads
        ga = scatter(ka + swap(sa, *C), ORDER_A)
        gb = scatter(kb + swap(sb, *C), ORDER_B)
        rest_sum = jnp.concatenate([ga[0], gb[0]], axis=0).astype(f32)
        d2 = grads[2][0] + swap(grads[3][0], *C)
        d0 = grads[0][0] + swap(grads[1][0], *C) + swap(d2, *X)
        triple_sum = scatter(d0, [Z1, Z0, Y])[0].astype(f32)
        tg2 = table_grads[2] + swap(table_grads[3], *C)
        tg = table_grads[0] + swap(table_grads[1], *C) + swap(tg2, *X)
        for step in (Y, Z0, Z1):
            tg = tg + swap(tg, *step)
        for step in (C, X, Y, Z0, Z1):
            sums2 = sums2 + swap(sums2, *step)
    else:
        sums1 = lax.psum(sums1, both)
        sums2 = lax.psum(sums2, both)
        peaks = lax.pmax(peaks[0], both)
        tg = lax.dynamic_slice_in_dim(lax.psum(jnp.concatenate(table_grads), both), me_mp * (HEADS // nmp), HEADS // nmp)
        reduce = lambda a, parts: lax.psum_scatter(
            uncanonical(a, parts, nmp, ndp).reshape(nmp * ndp, rows, -1), both, tiled=True)[0].astype(f32)
        triple_sum = reduce(jnp.concatenate([grads[k][0] for k in range(4)]), 3)
        rg = rest_grads[0]
        rest_sum = jnp.concatenate([reduce(rg[:, :, :128], 1), reduce(rg[:, :, 128:640], 1), reduce(rg[:, :, 640:], 1)], axis=1)

    flat_index = me_dp * nmp + me_mp
    count = ndp * nmp

    def piece(vector):
        width = vector.shape[0] // count
        return lax.dynamic_slice_in_dim(vector, flat_index * width, width)

    my_peaks = lax.dynamic_slice_in_dim(peaks, me_mp * (HEADS // nmp), HEADS // nmp)
    factor = clip_target / jnp.maximum(my_peaks, clip_target)
    clipped = triple_weight[:2] * jnp.repeat(jnp.sqrt(factor), HEAD_DIM)[None, None, :]
    wide = 512 * 4 // nmp
    return (result, dx, piece(sums2[0:512]), piece(sums2[512:1024]),
            triple_sum.reshape(rows, 3, own).transpose(1, 0, 2),
            piece(sums2[1024:1536]), piece(sums2[1536:2048]), tg,
            rest_sum[:, :own].T, piece(sums1[1536:2048]), piece(sums1[512:1024]), piece(sums1[1024:1536]),
            rest_sum[:, own:own + wide], piece(sums1[2048:4096]), rest_sum[:, own + wide:].T, piece(sums1[0:512]),
            my_peaks, clipped)


def solution(mesh):
    rows = P(("dp", "mp"), None)
    vector = P("dp")
    every = P(("dp", "mp"))
    three = P(None, "dp", "mp")
    down, across = P("mp", "dp"), P("dp", "mp")
    return jax.shard_map(
        shards,
        mesh=mesh,
        in_specs=(rows, P("dp", None), vector, vector, three, vector, vector, P("mp", None), down, vector, vector, vector,
                  across, vector, down, vector, rows),
        out_specs=(rows, rows, every, every, three, every, every, P("mp", None), down, every, every, every, across, every,
                   down, every, P("mp"), three),
        check_vma=False,
    )
```

time: 1650 us -> 406 us (0.25); the launches traced: 1630 us -> 399 us
  blocking collectives: 554 us -> 0 us
  matrix products: 380 us -> 6.28 us
  other arithmetic: 293 us -> 39.1 us
  Pallas kernels: 0 us -> 169 us
  waiting for transfers between devices: 181 us -> 38.2 us
  local copies, waits for them, and re-layouts: 198 us -> 97.1 us
  starting transfers between devices: 1.15 us -> 48 us
    all_gather x14 -> x0, blocking collectives: 493 us -> none  [the longest x9 344 us: combined_all(): lax.all_gather(a.astype(kind), axis)]
    dot_general x128 -> x6, matrix products: 380 us -> 6.28 us  [the longest x4 5.11 us: fold_table(): lax.dot_general(t, jnp.asarray(place_onehot()), (((1,), (1,)), ((), ())),...]
    pallas_call x0 -> x9, Pallas kernels: none -> 169 us  [the longest x4 69.8 us: attend_bwd(): pl.pallas_call(functools.partial(bwd_kernel, first, bool(last), blocks),...]
    convert_element_type x212 -> x6, other arithmetic: 168 us -> 4.87 us  [the longest x1 0.92 us: shards(): outer_weight.T.astype(bf)]
    reduce_scatter x8 -> x0, waiting for transfers between devices: 159 us -> none  [the longest x1 57.7 us: shards(): lax.psum_scatter(product(hidden, outer_here).astype(jnp.bfloat16), 'mp',...]
    unnamed x2 -> x0, blocking collectives: 60.9 us -> none
    ppermute x0 -> x50, starting transfers between devices: none -> 48 us  [swap(): lax.ppermute(x, axis, [(i, i ^ bit) for i in range(lax.axis_size(axis))])]
    ppermute x0 -> x50, waiting for transfers between devices: none -> 38.2 us  [swap(): lax.ppermute(x, axis, [(i, i ^ bit) for i in range(lax.axis_size(axis))])]
  transfers between devices with their start and end apart: 13 -> 50, of which waited for: 4 -> 13; matrix products, arithmetic and copies ran while one was open for 27% -> 30% of each run, Pallas kernels for 0% -> 31%
where the time goes in v1:
time: 406 us; the launch traced here: 399 us
  Pallas kernels  169 us (42%)
  local copies, waits for them, and re-layouts  97.1 us (24%)
  starting transfers between devices  48 us (12%)
  other arithmetic  39.1 us (10%)
  waiting for transfers between devices  38.2 us (9%)
  matrix products  6.28 us (2%)
    pallas_call x4, Pallas kernels, attend_bwd(): pl.pallas_call(functools.partial(bwd_kernel, first, bool(last), blocks),...  69.8 us
    pallas_call x4, Pallas kernels, attend_fwd(): pl.pallas_call(functools.partial(fwd_kernel, first, blocks), out_shape=ou...  52.7 us
    ppermute x50, starting transfers between devices, swap(): lax.ppermute(x, axis, [(i, i ^ bit) for i in range(lax.axis_size(axis))])  48 us
    pallas_call x1, Pallas kernels, mlp(): pl.pallas_call(functools.partial(mlp_kernel, (places, nblk, brow)), out_s...  46.1 us
    ppermute x50, waiting for transfers between devices, swap(): lax.ppermute(x, axis, [(i, i ^ bit) for i in range(lax.axis_size(axis))])  38.2 us
    unnamed x151, local copies, waits for them, and re-layouts  29.6 us
    reshape x8, local copies, waits for them, and re-layouts, fold_table(): t2[:, :PLACES, :15 * PLACES].reshape(n, PLACES, 15, PLACES)  17.2 us
    mul x2, local copies, waits for them, and re-layouts, spread_table(): t.reshape(n, 15, PLACES, PLACES).transpose(0, 2, 1, 3)  11.3 us
  transfers between devices with their start and end apart: 50, of which 13 were waited for; matrix products, arithmetic and copies ran while one was open for 30% of the time, Pallas kernels for 31%

profile of v1, /device:TPU:0, one launch (start us, length us, event | category | flops | bytes accessed | tf_op | source)
XLA Modules:
  0.0 399.4 jit_solution(15387519295713300653)
XLA Ops:
  9.5 3.6 collective-permute-start
  16.4 2.9 collective-permute-start.8
  26.2 4.6 %copy.89 = f32[16,49,15,49]{3,2,1,0:T(8,128)} copy(f32[16,49,15,49]{3,0,1,2:T(8,128)S(1)} %multiply_bitcast_fusion) | data formatting | bytes 4609920 | tf_op jit(solution)/shard_map/mul | solution.py:371
  30.9 6.7 %reshape.271 = f32[16,49,735]{2,1,0:T(8,128)} reshape(f32[16,49,15,49]{3,2,1,0:T(8,128)} %copy.89) | data formatting | bytes 4609920 | tf_op jit(solution)/shard_map/mul | solution.py:371
  37.6 2.0 pad_slice_fusion
  71.3 14.4 %shard_map.367 = (bf16[4,392,512]{2,1,0:T(8,128)(2,1)S(1)}, bf16[4,392,384]{2,1,0:T(8,128)(2,1)S(1)}, bf16[4,4,392,392]{3,2,1,0:T(8,128)(2,1)}, bf16[4,128,392]{...) custom-call(s32[1]{0:T(128)} %bitcast.refs_0_, ...), custom_call_target="tpu_custom_call" | custom-call | flops 8000000000 | bytes 16000000 | tf_op jit(solution)/shard_map/pallas_call | solution.py:133
  104.8 12.4 %shard_map.369 = (bf16[4,392,384]{2,1,0:T(8,128)(2,1)S(1)}, bf16[4,4,392,392]{3,2,1,0:T(8,128)(2,1)}, bf16[4,128,392]{2,1,0:T(8,128)(2,1)S(1)}, bf16[4,392,128]{...) custom-call(s32[1]{0:T(128)} %bitcast.refs_0_, ...), custom_call_target="tpu_custom_call" | custom-call | flops 8000000000 | bytes 16000000 | tf_op jit(solution)/shard_map/pallas_call | solution.py:133
  120.4 13.1 %shard_map.368 = (bf16[4,392,384]{2,1,0:T(8,128)(2,1)S(1)}, bf16[4,4,392,392]{3,2,1,0:T(8,128)(2,1)}, bf16[4,128,392]{2,1,0:T(8,128)(2,1)S(1)}, bf16[4,392,128]{...) custom-call(s32[1]{0:T(128)} %bitcast.refs_0_, ...), custom_call_target="tpu_custom_call" | custom-call | flops 8000000000 | bytes 16000000 | tf_op jit(solution)/shard_map/pallas_call | solution.py:133
  138.4 12.8 %shard_map.370 = (bf16[4,392,384]{2,1,0:T(8,128)(2,1)S(1)}, bf16[4,4,392,392]{3,2,1,0:T(8,128)(2,1)}, bf16[4,128,392]{2,1,0:T(8,128)(2,1)S(1)}, bf16[4,392,128]{...) custom-call(s32[1]{0:T(128)} %bitcast.refs_0_, ...), custom_call_target="tpu_custom_call" | custom-call | flops 8000000000 | bytes 16000000 | tf_op jit(solution)/shard_map/pallas_call | solution.py:133
  154.1 46.1 %shard_map.371 = (bf16[1568,512]{1,0:T(8,128)(2,1)}, f32[1568,512]{1,0:T(8,128)}, bf16[1568,512]{1,0:T(8,128)(2,1)}, bf16[4,512,128]{2,1,0:T(8,128)(2,1)}, f32[8...) custom-call(s32[1]{0:T(128)} %bitcast.refs_0_, ...), custom_call_target="tpu_custom_call" | custom-call | flops 25088000000 | bytes 30000000 | tf_op jit(solution)/shard_map/pallas_call | solution.py:351
  205.5 17.0 %shard_map.372 = (f32[4,392,512]{2,1,0:T(8,128)}, bf16[8,64,384]{2,1,0:T(8,128)(2,1)S(1)}, f32[4,56,768]{2,1,0:T(8,128)S(1)}, f32[8,128]{1,0:T(8,128)S(1)}) custom-call(s32[1]{0:T(128)} %bitcast.refs_0_, bf16[4,392,512]{2,1,0:T(8,128)(2,1)S(1)} %copy-done.17, bf16[4,392,384]{2,1,0:T(8,128)(2,1)S(1)} %copy-done.26, ...), custom_call_target="tpu_custom_call" | custom-call | flops 16000000000 | bytes 20000000 | tf_op jit(solution)/shard_map/pallas_call | solution.py:245
  222.6 17.2 %shard_map.373 = (f32[4,392,512]{2,1,0:T(8,128)}, bf16[8,64,384]{2,1,0:T(8,128)(2,1)S(1)}, f32[4,56,768]{2,1,0:T(8,128)S(1)}, f32[8,128]{1,0:T(8,128)S(1)}) custom-call(s32[1]{0:T(128)} %bitcast.refs_0_, bf16[4,392,512]{2,1,0:T(8,128)(2,1)S(1)} %copy-done.17, bf16[4,392,384]{2,1,0:T(8,128)(2,1)S(1)} %copy-done.22, ...), custom_call_target="tpu_custom_call" | custom-call | flops 16000000000 | bytes 20000000 | tf_op jit(solution)/shard_map/pallas_call | solution.py:245
  239.9 17.2 %shard_map.374 = (f32[4,392,512]{2,1,0:T(8,128)}, bf16[8,64,384]{2,1,0:T(8,128)(2,1)S(1)}, f32[4,56,768]{2,1,0:T(8,128)S(1)}, f32[8,128]{1,0:T(8,128)S(1)}) custom-call(s32[1]{0:T(128)} %bitcast.refs_0_, bf16[4,392,512]{2,1,0:T(8,128)(2,1)S(1)} %copy-done.18, bf16[4,392,384]{2,1,0:T(8,128)(2,1)S(1)} %copy-done.24, ...), custom_call_target="tpu_custom_call" | custom-call | flops 16000000000 | bytes 20000000 | tf_op jit(solution)/shard_map/pallas_call | solution.py:245
  257.1 18.4 %shard_map.375 = (bf16[4,392,512]{2,1,0:T(8,128)(2,1)}, bf16[8,64,384]{2,1,0:T(8,128)(2,1)S(1)}, f32[4,56,768]{2,1,0:T(8,128)S(1)}, f32[8,128]{1,0:T(8,128)S(1)}, f32[8,512]{1,0:T(8,128)S(1)}) custom-call(s32[1]{0:T(128)} %bitcast.refs_0_, bf16[4,392,512]{2,1,0:T(8,128)(2,1)S(1)} %copy-done.18, bf16[4,392,384]{2,1,0:T(8,128)(2,1)S(1)} %copy-done.20, ...), custom_call_target="tpu_custom_call" | custom-call | flops 16000000000 | bytes 20000000 | tf_op jit(solution)/shard_map/pallas_call | solution.py:245
  277.5 2.1 reshape.254
  279.6 2.6 copy.84
  286.2 3.1 reshape.251
  289.3 2.6 copy.82
  296.2 2.1 reshape.248
  298.3 2.6 copy.80
  300.9 2.1 reshape.249
  309.0 2.1 reshape.245
  311.1 2.7 copy.78
  327.4 2.7 collective-permute-start.49
  334.2 7.1 %collective-permute-done.25 = bf16[8,64,384]{2,1,0:T(8,128)(2,1)S(1)} collective-permute-done((bf16[8,64,384]{2,1,0:T(8,128)(2,1)S(1)}, bf16[8,64,384]{2,1,0:T(8,128)(2,1)S(1)}, u32[]{:S(2)}, u32[]{:S(2)}) %collective-permute-start.25) | collective-permute-done | bytes 393248 | tf_op jit(solution)/shard_map/ppermute | solution.py:382
  345.9 2.8 collective-permute-done.26
  354.5 3.0 collective-permute-start.28
  369.4 10.0 %collective-permute-done.41 = bf16[8,32,1152]{2,1,0:T(8,128)(2,1)S(1)} collective-permute-done((bf16[8,32,1152]{2,1,0:T(8,128)(2,1)}, bf16[8,32,1152]{2,1,0:T(8,128)(2,1)S(1)}, u32[]{:S(2)}, u32[]{:S(2)}) %collective-permute-start.41) | collective-permute-done | bytes 589856 | tf_op jit(solution)/shard_map/ppermute | solution.py:382
  383.3 3.0 collective-permute-done.42
  388.8 3.0 collective-permute-done.43
  392.0 2.8 collective-permute-done.39
  394.8 3.0 collective-permute-done.44
  (402 shorter events, 149.6 us)
Async XLA Ops:
  1.5 19.2 %collective-permute-start.3 = (bf16[4,2535]{1,0:T(4,128)(2,1)S(1)}, bf16[4,2535]{1,0:T(4,128)(2,1)S(1)}, u32[]{:S(2)}, u32[]{:S(2)}) collective-permute-start(bf16[4,2535]{1,0:T(4,128)(2,1)S(1)} %convert_element_type.68), channel_id=1, source_target_pairs={{0,1},{1,0},{2,3},{3,2},{4,5},{5,4},{6,7},{7,6},{8,9},{9,8},{10,11... | collective-permute-start | bytes 60848 | tf_op jit(solution)/shard_map/ppermute | solution.py:382
  9.5 30.0 %collective-permute-start = (bf16[1,80,384]{2,1,0:T(8,128)(2,1)}, bf16[1,80,384]{2,1,0:T(8,128)(2,1)}, u32[]{:S(2)}, u32[]{:S(2)}) collective-permute-start(bf16[1,80,384]{2,1,0:T(8,128)(2,1)} %maximum_bitcast_fusion), channel_id=1, source_target_pairs={{0,16},{4,20},{8,24},{12,28},{16,0},{20,4},{24,8},{28,12},{1,17},{... | collective-permute-start | bytes 184328 | tf_op jit(solution)/shard_map/ppermute | solution.py:382
  16.4 25.7 %collective-permute-start.13 = (bf16[1,32,1152]{2,1,0:T(8,128)(2,1)}, bf16[1,32,1152]{2,1,0:T(8,128)(2,1)}, u32[]{:S(2)}, u32[]{:S(2)}) collective-permute-start(bf16[1,32,1152]{2,1,0:T(8,128)(2,1)} %get-tuple-element.178), channel_id=1, source_target_pairs={{0,16},{4,20},{8,24},{12,28},{16,0},{20,4},{24,8},{28,12},{1,17},{... | collective-permute-start | bytes 221192 | tf_op jit(solution)/shard_map/ppermute | solution.py:382
  16.4 27.1 %collective-permute-start.8 = (bf16[1,32,1152]{2,1,0:T(8,128)(2,1)}, bf16[1,32,1152]{2,1,0:T(8,128)(2,1)}, u32[]{:S(2)}, u32[]{:S(2)}) collective-permute-start(bf16[1,32,1152]{2,1,0:T(8,128)(2,1)} %get-tuple-element.179), channel_id=1, source_target_pairs={{0,16},{4,20},{8,24},{12,28},{16,0},{20,4},{24,8},{28,12},{1,17},{... | collective-permute-start | bytes 221192 | tf_op jit(solution)/shard_map/ppermute | solution.py:382
  40.4 8.7 %collective-permute-start.1 = (bf16[2,80,384]{2,1,0:T(8,128)(2,1)S(1)}, bf16[2,80,384]{2,1,0:T(8,128)(2,1)S(1)}, u32[]{:S(2)}, u32[]{:S(2)}) collective-permute-start(bf16[2,80,384]{2,1,0:T(8,128)(2,1)S(1)} %pad_maximum_fusion.11), channel_id=1, source_target_pairs={{0,8},{4,12},{8,0},{12,4},{16,24},{20,28},{24,16},{28,20},{1,9},{5... | collective-permute-start | bytes 368648 | tf_op jit(solution)/shard_map/ppermute | solution.py:382
  44.5 10.4 %collective-permute-start.9 = (bf16[2,32,1152]{2,1,0:T(8,128)(2,1)S(1)}, bf16[2,32,1152]{2,1,0:T(8,128)(2,1)S(1)}, u32[]{:S(2)}, u32[]{:S(2)}) collective-permute-start(bf16[2,32,1152]{2,1,0:T(8,128)(2,1)S(1)} %pad_maximum_fusion.9), channel_id=1, source_target_pairs={{0,8},{4,12},{8,0},{12,4},{16,24},{20,28},{24,16},{28,20},{1,9},{5... | collective-permute-start | bytes 442376 | tf_op jit(solution)/shard_map/ppermute | solution.py:382
  53.4 42.5 %collective-permute-start.15 = (bf16[4,32,1152]{2,1,0:T(8,128)(2,1)}, bf16[4,32,1152]{2,1,0:T(8,128)(2,1)}, u32[]{:S(2)}, u32[]{:S(2)}) collective-permute-start(bf16[4,32,1152]{2,1,0:T(8,128)(2,1)} %pad_maximum_fusion.6), channel_id=1, source_target_pairs={{0,2},{1,3},{2,0},{3,1},{4,6},{5,7},{6,4},{7,5},{8,10},{9,11},{10,... | collective-permute-start | bytes 884744 | tf_op jit(solution)/shard_map/ppermute | solution.py:382
  56.6 42.1 %collective-permute-start.10 = (bf16[4,32,1152]{2,1,0:T(8,128)(2,1)}, bf16[4,32,1152]{2,1,0:T(8,128)(2,1)}, u32[]{:S(2)}, u32[]{:S(2)}) collective-permute-start(bf16[4,32,1152]{2,1,0:T(8,128)(2,1)} %pad_maximum_fusion.5), channel_id=1, source_target_pairs={{0,4},{4,0},{8,12},{12,8},{16,20},{20,16},{24,28},{28,24},{1,5},{5... | collective-permute-start | bytes 884744 | tf_op jit(solution)/shard_map/ppermute | solution.py:382
  69.9 50.4 %collective-permute-start.5 = (bf16[8,64,384]{2,1,0:T(8,128)(2,1)}, bf16[8,64,384]{2,1,0:T(8,128)(2,1)}, u32[]{:S(2)}, u32[]{:S(2)}) collective-permute-start(bf16[8,64,384]{2,1,0:T(8,128)(2,1)} %pad_maximum_fusion.2.refs_3_), channel_id=1, source_target_pairs={{0,1},{1,0},{2,3},{3,2},{4,5},{5,4},{6,7},{7,6},{8,9},{9,8},{10,11... | collective-permute-start | bytes 1179656 | tf_op jit(solution)/shard_map/ppermute | solution.py:382
  92.3 12.4 %collective-permute-start.6 = (bf16[8,64,384]{2,1,0:T(8,128)(2,1)}, bf16[8,64,384]{2,1,0:T(8,128)(2,1)S(1)}, u32[]{:S(2)}, u32[]{:S(2)}) collective-permute-start(bf16[8,64,384]{2,1,0:T(8,128)(2,1)} %pad_maximum_fusion.2.refs_3_), channel_id=1, source_target_pairs={{0,2},{1,3},{2,0},{3,1},{4,6},{5,7},{6,4},{7,5},{8,10},{9,11},{10,... | collective-permute-start | bytes 1179656 | tf_op jit(solution)/shard_map/ppermute | solution.py:382
  97.1 22.3 %collective-permute-start.16 = (bf16[8,32,1152]{2,1,0:T(8,128)(2,1)S(1)}, bf16[8,32,1152]{2,1,0:T(8,128)(2,1)S(1)}, u32[]{:S(2)}, u32[]{:S(2)}) collective-permute-start(bf16[8,32,1152]{2,1,0:T(8,128)(2,1)S(1)} %pad_maximum_fusion.1), channel_id=1, source_target_pairs={{0,4},{4,0},{8,12},{12,8},{16,20},{20,16},{24,28},{28,24},{1,5},{5... | collective-permute-start | bytes 1769480 | tf_op jit(solution)/shard_map/ppermute | solution.py:382
  99.8 18.2 %collective-permute-start.11 = (bf16[8,32,1152]{2,1,0:T(8,128)(2,1)S(1)}, bf16[8,32,1152]{2,1,0:T(8,128)(2,1)S(1)}, u32[]{:S(2)}, u32[]{:S(2)}) collective-permute-start(bf16[8,32,1152]{2,1,0:T(8,128)(2,1)S(1)} %pad_maximum_fusion), channel_id=1, source_target_pairs={{0,2},{1,3},{2,0},{3,1},{4,6},{5,7},{6,4},{7,5},{8,10},{9,11},{10,... | collective-permute-start | bytes 1769480 | tf_op jit(solution)/shard_map/ppermute | solution.py:382
  104.8 32.2 %collective-permute-start.7 = (bf16[8,64,384]{2,1,0:T(8,128)(2,1)S(1)}, bf16[8,64,384]{2,1,0:T(8,128)(2,1)}, u32[]{:S(2)}, u32[]{:S(2)}) collective-permute-start(bf16[8,64,384]{2,1,0:T(8,128)(2,1)S(1)} %collective-permute-done.6.refs_2_), channel_id=1, source_target_pairs={{0,1},{1,0},{2,3},{3,2},{4,5},{5,4},{6,7},{7,6},{8,9},{9,8},{10,11... | collective-permute-start | bytes 1179656 | tf_op jit(solution)/shard_map/ppermute | solution.py:382
  118.9 35.1 %collective-permute-start.12 = (bf16[16,32,1152]{2,1,0:T(8,128)(2,1)}, bf16[16,32,1152]{2,1,0:T(8,128)(2,1)}, u32[]{:S(2)}, u32[]{:S(2)}) collective-permute-start(bf16[16,32,1152]{2,1,0:T(8,128)(2,1)} %constant_dynamic-update-slice_fusion.refs_9_), channel_id=1, source_target_pairs={{0,1},{1,0},{2,3},{3,2},{4,5},{5,4},{6,7},{7,6},{8,9},{9,8},{10,11... | collective-permute-start | bytes 3538952 | tf_op jit(solution)/shard_map/ppermute | solution.py:382
  120.3 33.8 %collective-permute-start.17 = (bf16[16,32,1152]{2,1,0:T(8,128)(2,1)}, bf16[16,32,1152]{2,1,0:T(8,128)(2,1)}, u32[]{:S(2)}, u32[]{:S(2)}) collective-permute-start(bf16[16,32,1152]{2,1,0:T(8,128)(2,1)} %constant_dynamic-update-slice_fusion.5.refs_11_), channel_id=1, source_target_pairs={{0,1},{1,0},{2,3},{3,2},{4,5},{5,4},{6,7},{7,6},{8,9},{9,8},{10,11... | collective-permute-start | bytes 3538952 | tf_op jit(solution)/shard_map/ppermute | solution.py:382
  202.6 101.8 %collective-permute-start.45 = (f32[33,128]{1,0:T(8,128)}, f32[33,128]{1,0:T(8,128)}, u32[]{:S(2)}, u32[]{:S(2)}) collective-permute-start(f32[33,128]{1,0:T(8,128)} %fusion.4), channel_id=1, source_target_pairs={{0,1},{1,0},{2,3},{3,2},{4,5},{5,4},{6,7},{7,6},{8,9},{9,8},{10,11... | collective-permute-start | bytes 50696 | tf_op jit(solution)/shard_map/ppermute | solution.py:382
  275.7 18.1 %collective-permute-start.18 = (f32[2048]{0:T(1024)S(1)}, f32[2048]{0:T(1024)S(1)}, u32[]{:S(2)}, u32[]{:S(2)}) collective-permute-start(f32[2048]{0:T(1024)S(1)} %pad_maximum_fusion.15), channel_id=1, source_target_pairs={{0,1},{1,0},{2,3},{3,2},{4,5},{5,4},{6,7},{7,6},{8,9},{9,8},{10,11... | collective-permute-start | bytes 24584 | tf_op jit(solution)/shard_map/ppermute | solution.py:382
  276.9 57.3 %collective-permute-start.23 = (bf16[8,64,384]{2,1,0:T(8,128)(2,1)S(1)}, bf16[8,64,384]{2,1,0:T(8,128)(2,1)}, u32[]{:S(2)}, u32[]{:S(2)}) collective-permute-start(bf16[8,64,384]{2,1,0:T(8,128)(2,1)S(1)} %get-tuple-element.113), channel_id=1, source_target_pairs={{0,1},{1,0},{2,3},{3,2},{4,5},{5,4},{6,7},{7,6},{8,9},{9,8},{10,11... | collective-permute-start | bytes 1179656 | tf_op jit(solution)/shard_map/ppermute | solution.py:382
  277.4 48.8 %collective-permute-start.24 = (bf16[8,64,384]{2,1,0:T(8,128)(2,1)S(1)}, bf16[8,64,384]{2,1,0:T(8,128)(2,1)}, u32[]{:S(2)}, u32[]{:S(2)}) collective-permute-start(bf16[8,64,384]{2,1,0:T(8,128)(2,1)S(1)} %get-tuple-element.115), channel_id=1, source_target_pairs={{0,1},{1,0},{2,3},{3,2},{4,5},{5,4},{6,7},{7,6},{8,9},{9,8},{10,11... | collective-permute-start | bytes 1179656 | tf_op jit(solution)/shard_map/ppermute | solution.py:382
  285.7 33.1 %collective-permute-start.30 = (f32[4,2535]{1,0:T(4,128)S(1)}, f32[4,2535]{1,0:T(4,128)S(1)}, u32[]{:S(2)}, u32[]{:S(2)}) collective-permute-start(f32[4,2535]{1,0:T(4,128)S(1)} %reshape.256), channel_id=1, source_target_pairs={{0,1},{1,0},{2,3},{3,2},{4,5},{5,4},{6,7},{7,6},{8,9},{9,8},{10,11... | collective-permute-start | bytes 121688 | tf_op jit(solution)/shard_map/ppermute | solution.py:382
  293.8 9.3 %collective-permute-start.19 = (f32[2048]{0:T(1024)S(1)}, f32[2048]{0:T(1024)S(1)}, u32[]{:S(2)}, u32[]{:S(2)}) collective-permute-start(f32[2048]{0:T(1024)S(1)} %fusion.10), channel_id=1, source_target_pairs={{0,2},{1,3},{2,0},{3,1},{4,6},{5,7},{6,4},{7,5},{8,10},{9,11},{10,... | collective-permute-start | bytes 24584 | tf_op jit(solution)/shard_map/ppermute | solution.py:382
  305.2 10.9 %collective-permute-start.46 = (f32[33,128]{1,0:T(8,128)S(1)}, f32[33,128]{1,0:T(8,128)S(1)}, u32[]{:S(2)}, u32[]{:S(2)}) collective-permute-start(f32[33,128]{1,0:T(8,128)S(1)} %add_select_fusion.4), channel_id=1, source_target_pairs={{0,2},{1,3},{2,0},{3,1},{4,6},{5,7},{6,4},{7,5},{8,10},{9,11},{10,... | collective-permute-start | bytes 50696 | tf_op jit(solution)/shard_map/ppermute | solution.py:382
  306.8 8.9 %collective-permute-start.21 = (f32[2048]{0:T(1024)S(1)}, f32[2048]{0:T(1024)S(1)}, u32[]{:S(2)}, u32[]{:S(2)}) collective-permute-start(f32[2048]{0:T(1024)S(1)} %add.135), channel_id=1, source_target_pairs={{0,8},{4,12},{8,0},{12,4},{16,24},{20,28},{24,16},{28,20},{1,9},{5... | collective-permute-start | bytes 24584 | tf_op jit(solution)/shard_map/ppermute | solution.py:382
  320.3 30.0 %collective-permute-start.35 = (bf16[16,32,1152]{2,1,0:T(8,128)(2,1)}, bf16[16,32,1152]{2,1,0:T(8,128)(2,1)S(1)}, u32[]{:S(2)}, u32[]{:S(2)}) collective-permute-start(bf16[16,32,1152]{2,1,0:T(8,128)(2,1)} %get-tuple-element.121), channel_id=1, source_target_pairs={{0,1},{1,0},{2,3},{3,2},{4,5},{5,4},{6,7},{7,6},{8,9},{9,8},{10,11... | collective-permute-start | bytes 3538952 | tf_op jit(solution)/shard_map/ppermute | solution.py:382
  326.2 34.8 %collective-permute-start.40 = (bf16[16,32,1152]{2,1,0:T(8,128)(2,1)}, bf16[16,32,1152]{2,1,0:T(8,128)(2,1)}, u32[]{:S(2)}, u32[]{:S(2)}) collective-permute-start(bf16[16,32,1152]{2,1,0:T(8,128)(2,1)} %get-tuple-element.123), channel_id=1, source_target_pairs={{0,1},{1,0},{2,3},{3,2},{4,5},{5,4},{6,7},{7,6},{8,9},{9,8},{10,11... | collective-permute-start | bytes 3538952 | tf_op jit(solution)/shard_map/ppermute | solution.py:382
  330.1 11.2 %collective-permute-start.25 = (bf16[8,64,384]{2,1,0:T(8,128)(2,1)S(1)}, bf16[8,64,384]{2,1,0:T(8,128)(2,1)S(1)}, u32[]{:S(2)}, u32[]{:S(2)}) collective-permute-start(bf16[8,64,384]{2,1,0:T(8,128)(2,1)S(1)} %add.141), channel_id=1, source_target_pairs={{0,2},{1,3},{2,0},{3,1},{4,6},{5,7},{6,4},{7,5},{8,10},{9,11},{10,... | collective-permute-start | bytes 1179656 | tf_op jit(solution)/shard_map/ppermute | solution.py:382
  332.2 12.2 %collective-permute-start.32 = (f32[4,2535]{1,0:T(4,128)S(1)}, f32[4,2535]{1,0:T(4,128)S(1)}, u32[]{:S(2)}, u32[]{:S(2)}) collective-permute-start(f32[4,2535]{1,0:T(4,128)S(1)} %add_add_fusion.1), channel_id=1, source_target_pairs={{0,4},{4,0},{8,12},{12,8},{16,20},{20,16},{24,28},{28,24},{1,5},{5... | collective-permute-start | bytes 121688 | tf_op jit(solution)/shard_map/ppermute | solution.py:382
  350.3 10.1 %collective-permute-start.34 = (f32[4,2535]{1,0:T(4,128)S(1)}, f32[4,2535]{1,0:T(4,128)S(1)}, u32[]{:S(2)}, u32[]{:S(2)}) collective-permute-start(f32[4,2535]{1,0:T(4,128)S(1)} %add.150), channel_id=1, source_target_pairs={{0,16},{4,20},{8,24},{12,28},{16,0},{20,4},{24,8},{28,12},{1,17},{... | collective-permute-start | bytes 121688 | tf_op jit(solution)/shard_map/ppermute | solution.py:382
  353.9 14.6 %collective-permute-start.36 = (bf16[8,32,1152]{2,1,0:T(8,128)(2,1)}, bf16[8,32,1152]{2,1,0:T(8,128)(2,1)S(1)}, u32[]{:S(2)}, u32[]{:S(2)}) collective-permute-start(bf16[8,32,1152]{2,1,0:T(8,128)(2,1)} %slice.327), channel_id=1, source_target_pairs={{0,2},{1,3},{2,0},{3,1},{4,6},{5,7},{6,4},{7,5},{8,10},{9,11},{10,... | collective-permute-start | bytes 1769480 | tf_op jit(solution)/shard_map/ppermute | solution.py:382
  354.5 10.2 %collective-permute-start.28 = (bf16[1,64,384]{2,1,0:T(8,128)(2,1)S(1)}, bf16[1,64,384]{2,1,0:T(8,128)(2,1)S(1)}, u32[]{:S(2)}, u32[]{:S(2)}) collective-permute-start(bf16[1,64,384]{2,1,0:T(8,128)(2,1)S(1)} %slice.323), channel_id=1, source_target_pairs={{0,16},{4,20},{8,24},{12,28},{16,0},{20,4},{24,8},{28,12},{1,17},{... | collective-permute-start | bytes 147464 | tf_op jit(solution)/shard_map/ppermute | solution.py:382
  363.4 16.0 %collective-permute-start.41 = (bf16[8,32,1152]{2,1,0:T(8,128)(2,1)}, bf16[8,32,1152]{2,1,0:T(8,128)(2,1)S(1)}, u32[]{:S(2)}, u32[]{:S(2)}) collective-permute-start(bf16[8,32,1152]{2,1,0:T(8,128)(2,1)} %slice.335), channel_id=1, source_target_pairs={{0,4},{4,0},{8,12},{12,8},{16,20},{20,16},{24,28},{28,24},{1,5},{5... | collective-permute-start | bytes 1769480 | tf_op jit(solution)/shard_map/ppermute | solution.py:382
  368.5 14.0 %collective-permute-start.37 = (bf16[4,32,1152]{2,1,0:T(8,128)(2,1)S(1)}, bf16[4,32,1152]{2,1,0:T(8,128)(2,1)S(1)}, u32[]{:S(2)}, u32[]{:S(2)}) collective-permute-start(bf16[4,32,1152]{2,1,0:T(8,128)(2,1)S(1)} %slice.329), channel_id=1, source_target_pairs={{0,4},{4,0},{8,12},{12,8},{16,20},{20,16},{24,28},{28,24},{1,5},{5... | collective-permute-start | bytes 884744 | tf_op jit(solution)/shard_map/ppermute | solution.py:382
  (86 other events, 782.2 us)
